TPU v7x, 128 devices: a whole 4x4x4 slice. The times are simulated.
128 devices in a mesh: seq: 16 (over y_lo, x, core), fsdp: 8 (over y_hi, z).
Axes of the slice: x: 4, y: 4 (y_hi: 2, y_lo: 2; y = y_hi * 2 + y_lo), z: 4, core: 2. Of those that a mesh axis runs over, the one named last changes fastest.
Arguments:
- inputs: bfloat16 [8, 2048, 1024], P('fsdp', 'seq'), may hold values from -6 to 6
- cotangent: bfloat16 [8, 2048, 1024], P('fsdp', 'seq'), may hold values from -6 to 6
- lengths: int32 [8], P('fsdp'), may hold values from 512 to 2048, as said below
- mixer_gain: bfloat16 [1024], P('fsdp'), may hold values from 0.099609375 to 1.8984375
- mixer_input: bfloat16 [1024, 1024], P('fsdp'), may hold values from -0.1875 to 0.1875
- mixer_gate: bfloat16 [1024, 1024], P('fsdp'), may hold values from -0.1875 to 0.1875
- mixer_kernel: bfloat16 [3, 1024], P(None, 'fsdp'), may hold values from -3.5 to 3.5
- lower_gain: bfloat16 [1024], P('fsdp'), may hold values from 0.099609375 to 1.8984375
- lower_gate: bfloat16 [1024, 2048], P('fsdp'), may hold values from -0.1875 to 0.1875
- lower_up: bfloat16 [1024, 2048], P('fsdp'), may hold values from -0.1875 to 0.1875
- lower_down: bfloat16 [2048, 1024], P('fsdp'), may hold values from -0.125 to 0.125
- attention_gain: bfloat16 [1024], P('fsdp'), may hold values from 0.099609375 to 1.8984375
- attention_query: bfloat16 [1024, 1024], P('fsdp'), may hold values from -0.1875 to 0.1875
- attention_key: bfloat16 [1024, 1024], P('fsdp'), may hold values from -0.1875 to 0.1875
- attention_value: bfloat16 [1024, 1024], P('fsdp'), may hold values from -0.1875 to 0.1875
- attention_output: bfloat16 [1024, 1024], P('fsdp'), may hold values from -0.75 to 0.75
- upper_gain: bfloat16 [1024], P('fsdp'), may hold values from 0.099609375 to 1.8984375
- upper_gate: bfloat16 [1024, 2048], P('fsdp'), may hold values from -0.1875 to 0.1875
- upper_up: bfloat16 [1024, 2048], P('fsdp'), may hold values from -0.1875 to 0.1875
- upper_down: bfloat16 [2048, 1024], P('fsdp'), may hold values from -0.125 to 0.125
Outputs:
- outputs: bfloat16 [8, 2048, 1024], P('fsdp', 'seq')
- input_grad: float32 [8, 2048, 1024], P('fsdp', 'seq')
- grad_mixer_gain: float32 [1024], P('fsdp')
- grad_mixer_input: float32 [1024, 1024], P('fsdp')
- grad_mixer_gate: float32 [1024, 1024], P('fsdp')
- grad_mixer_kernel: float32 [3, 1024], P(None, 'fsdp')
- grad_lower_gain: float32 [1024], P('fsdp')
- grad_lower_gate: float32 [1024, 2048], P('fsdp')
- grad_lower_up: float32 [1024, 2048], P('fsdp')
- grad_lower_down: float32 [2048, 1024], P('fsdp')
- grad_attention_gain: float32 [1024], P('fsdp')
- grad_attention_query: float32 [1024, 1024], P('fsdp')
- grad_attention_key: float32 [1024, 1024], P('fsdp')
- grad_attention_value: float32 [1024, 1024], P('fsdp')
- grad_attention_output: float32 [1024, 1024], P('fsdp')
- grad_upper_gain: float32 [1024], P('fsdp')
- grad_upper_gate: float32 [1024, 2048], P('fsdp')
- grad_upper_up: float32 [1024, 2048], P('fsdp')
- grad_upper_down: float32 [2048, 1024], P('fsdp')
Inputs may be any that keep to these rules, and one draw needn't show every extreme that they name: lengths[s] is the number of valid slots of sequence s; its slots from lengths[s] on are padding. At least one sequence fills all 2048 slots.
All inputs are finite; a program needn't handle non-finite values.
Results may differ from a plain program's by a relative error of at most 0.025.
Values may be sent and summed in bfloat16 or wider, within the bound.
No kernel may reach another device: no remote copies, remote signals or barrier semaphores. Data moves between devices by JAX's collectives and lax.ppermute only.
A program may use at most 192 MiB of HBM per device.

v0:
```python
import jax
import jax.numpy as jnp
from jax import lax
from jax.sharding import PartitionSpec as P

HEADS = 16
HEAD_DIM = 64
WINDOW = 64


EPSILON = 1e-05
MASKED_SCORE = -1e30


def for_sending(value):
    return jax.tree.map(lambda a: a.astype(jnp.bfloat16) if a.dtype == jnp.float32 else a, value)


def from_behind(value, axis, by):
    size = lax.axis_size(axis)
    pairs = [(i, i + by) for i in range(size) if 0 <= i + by < size]
    return lax.ppermute(value, axis, pairs)


def product(left, right):
    return jnp.dot(left, right, preferred_element_type=jnp.float32)


def weight_product(left, right):
    return lax.dot_general(
        left, right, (((0,), (0,)), ((), ())), preferred_element_type=jnp.float32
    )


def input_product(left, right):
    return lax.dot_general(
        left, right, (((1,), (1,)), ((), ())), preferred_element_type=jnp.float32
    )


def normalize(stream, norm_gain):
    row_scale = lax.rsqrt(jnp.mean(stream * stream, axis=-1, keepdims=True) + EPSILON)
    return ((stream * row_scale * norm_gain).astype(jnp.bfloat16), row_scale)


def norm_back(stream, row_scale, norm_gain, upstream):
    weighted = upstream * norm_gain
    row_inner = jnp.mean(weighted * stream, axis=-1, keepdims=True)
    grad_stream = row_scale * (weighted - stream * row_scale * row_scale * row_inner)
    grad_gain = jnp.sum(upstream * stream * row_scale, axis=0)
    return (grad_stream, grad_gain)


def add_tail(own_rows, tail_rows):
    keep_count = own_rows.shape[0] - tail_rows.shape[0]
    return jnp.concatenate([own_rows[:keep_count], own_rows[keep_count:] + tail_rows], axis=0)


def convolve(kernel, extended):
    return kernel[0] * extended[2:] + kernel[1] * extended[1:-1] + kernel[2] * extended[:-2]


def mixer_local(stream, weights):
    norm_gain, input_matrix, gate_matrix, kernel_columns = weights
    normed, row_scale = normalize(stream, norm_gain.astype(jnp.float32))
    signal = product(normed, input_matrix).astype(jnp.bfloat16)
    gate_act = product(normed, gate_matrix)
    return (normed, row_scale, signal, gate_act)


def swiglu_local(stream, weights):
    norm_gain, gate_matrix, up_matrix, down_matrix = weights
    normed, row_scale = normalize(stream, norm_gain.astype(jnp.float32))
    gate_act = product(normed, gate_matrix)
    upward = product(normed, up_matrix)
    hidden = (jax.nn.silu(gate_act) * upward).astype(jnp.bfloat16)
    return (normed, row_scale, gate_act, upward, hidden)


def project_heads(stream, weights):
    norm_gain, query_matrix, key_matrix, value_matrix, output_matrix = weights
    normed, row_scale = normalize(stream, norm_gain.astype(jnp.float32))
    query = product(normed, query_matrix).astype(jnp.bfloat16)
    keys = product(normed, key_matrix).astype(jnp.bfloat16)
    values = product(normed, value_matrix).astype(jnp.bfloat16)
    return (normed, row_scale, query, keys, values)


def body(
    inputs,
    cotangent,
    lengths,
    mixer_gain,
    mixer_input,
    mixer_gate,
    mixer_kernel,
    lower_gain,
    lower_gate,
    lower_up,
    lower_down,
    attention_gain,
    attention_query,
    attention_key,
    attention_value,
    attention_output,
    upper_gain,
    upper_gate,
    upper_up,
    upper_down,
):
    row_count = inputs.shape[1]
    model_width = inputs.shape[2]
    reach_rows = WINDOW - 1
    block_rows = min(row_count, 512)
    block_count = row_count // block_rows
    base_row = lax.axis_index("seq") * row_count
    starts_all = jnp.arange(block_count, dtype=jnp.int32) * block_rows
    score_scale = HEAD_DIM ** (-0.5)

    def fetch(parts):
        return jax.tree.map(
            lambda part, own: part.astype(own.dtype),
            lax.all_gather(for_sending(parts), "fsdp", axis=0, tiled=True),
            parts,
        )

    def settle(parts):
        shares = jax.tree.map(
            lambda part: part.astype(jnp.float32),
            lax.psum_scatter(for_sending(parts), "fsdp", scatter_dimension=0, tiled=True),
        )
        return jax.tree.map(
            lambda part: part.astype(jnp.float32), lax.psum(for_sending(shares), "seq")
        )

    def masked_scores(query_heads, keys_ext, block_start):
        scores = (
            jnp.einsum("qhd,khd->hqk", query_heads, keys_ext, preferred_element_type=jnp.float32)
            * score_scale
        )
        query_place = base_row + block_start + jnp.arange(block_rows, dtype=jnp.int32)
        key_place = (
            base_row
            + block_start
            - reach_rows
            + jnp.arange(block_rows + reach_rows, dtype=jnp.int32)
        )
        allowed = (
            (key_place[None, :] <= query_place[:, None])
            & (key_place[None, :] > query_place[:, None] - WINDOW)
            & (key_place[None, :] >= 0)
        )
        return (jnp.where(allowed[None], scores, MASKED_SCORE), query_heads, keys_ext)

    def swiglu_back(stream, weights, grad_out, saved):
        normed, row_scale, gate_act, upward, hidden = saved
        norm_gain, gate_matrix, up_matrix, down_matrix = weights
        grad_branch = grad_out.astype(jnp.bfloat16)
        grad_down = weight_product(hidden, grad_branch)
        grad_hidden = input_product(grad_branch, down_matrix)
        sigmoid_gate = jax.nn.sigmoid(gate_act)
        grad_gate = (
            grad_hidden * upward * sigmoid_gate * (1.0 + gate_act * (1.0 - sigmoid_gate))
        ).astype(jnp.bfloat16)
        grad_up = (grad_hidden * jax.nn.silu(gate_act)).astype(jnp.bfloat16)
        grad_gate_matrix = weight_product(normed, grad_gate)
        grad_up_matrix = weight_product(normed, grad_up)
        grad_normed = input_product(grad_gate, gate_matrix) + input_product(grad_up, up_matrix)
        grad_stream, grad_gain = norm_back(
            stream, row_scale, norm_gain.astype(jnp.float32), grad_normed
        )
        return (grad_out + grad_stream, (grad_gain, grad_gate_matrix, grad_up_matrix, grad_down))

    start_stream = inputs[0].astype(jnp.float32)
    mixer_parts = (mixer_gain, mixer_input, mixer_gate, mixer_kernel.T)
    mixer_full = fetch(mixer_parts)
    mixer_normed, mixer_scale, signal, gate_act = mixer_local(start_stream, mixer_full)
    conv_edge = from_behind(signal[row_count - 2 :], "seq", 1)
    extended = jnp.concatenate([conv_edge, signal], axis=0).astype(jnp.float32)
    conv_out = convolve(mixer_full[3].T.astype(jnp.float32), extended)
    mixed_stream = start_stream + conv_out * gate_act
    lower_parts = (lower_gain, lower_gate, lower_up, lower_down)
    lower_full = fetch(lower_parts)
    lower_saved = swiglu_local(mixed_stream, lower_full)
    lower_stream = mixed_stream + product(lower_saved[4], lower_full[3])
    attention_parts = (
        attention_gain,
        attention_query,
        attention_key,
        attention_value,
        attention_output,
    )
    attention_full = fetch(attention_parts)
    attention_normed, attention_scale, query, keys, values = project_heads(
        lower_stream, attention_full
    )
    key_edge, value_edge = from_behind(
        (keys[row_count - reach_rows :], values[row_count - reach_rows :]), "seq", 1
    )
    head_query_heads = query.reshape(row_count, HEADS, HEAD_DIM)
    head_keys_ext = jnp.concatenate([key_edge, keys], axis=0).reshape(
        row_count + reach_rows, HEADS, HEAD_DIM
    )
    head_values_ext = jnp.concatenate([value_edge, values], axis=0).reshape(
        row_count + reach_rows, HEADS, HEAD_DIM
    )
    query_heads = head_query_heads
    keys_ext = head_keys_ext

    def attend(block_start):
        scores, query_piece, key_piece = masked_scores(query_heads, keys_ext, block_start)
        row_max = jnp.max(scores, axis=-1, keepdims=True)
        shifted = jnp.exp(scores - row_max)
        row_total = jnp.sum(shifted, axis=-1, keepdims=True)
        probability = (shifted / row_total).astype(jnp.bfloat16)
        block_out = jnp.einsum(
            "hqk,khd->qhd", probability, head_values_ext, preferred_element_type=jnp.float32
        )
        return (block_out, (row_max + jnp.log(row_total))[..., 0])

    block_outs, log_totals = lax.map(attend, starts_all)
    attended = block_outs.reshape(row_count, model_width).astype(jnp.bfloat16)
    attended_stream = lower_stream + product(attended, attention_full[4])
    upper_parts = (upper_gain, upper_gate, upper_up, upper_down)
    upper_full = fetch(upper_parts)
    upper_saved = swiglu_local(attended_stream, upper_full)
    final_stream = attended_stream + product(upper_saved[4], upper_full[3])
    valid = (base_row + jnp.arange(row_count, dtype=jnp.int32) < lengths[0]).astype(jnp.float32)
    grad_stream = cotangent[0].astype(jnp.float32) * valid[:, None]
    grad_stream, upper_grads = swiglu_back(attended_stream, upper_full, grad_stream, upper_saved)
    upper_done = settle(upper_grads)
    grad_out = grad_stream
    normed = attention_normed
    row_scale = attention_scale
    attention_query_heads = query_heads
    attention_keys_ext = keys_ext
    norm_gain, query_matrix, key_matrix, value_matrix, output_matrix = attention_full
    grad_branch = grad_out.astype(jnp.bfloat16)
    grad_output_matrix = weight_product(attended, grad_branch)
    grad_attended = (
        input_product(grad_branch, output_matrix)
        .astype(jnp.bfloat16)
        .reshape(row_count, HEADS, HEAD_DIM)
    )

    def back_block(carried, block_item):
        grad_keys_ext, grad_values_ext = carried
        block_start, log_block = block_item
        scores, query_piece, key_piece = masked_scores(
            attention_query_heads, attention_keys_ext, block_start
        )
        probability = jnp.exp(scores - log_block[..., None])
        grad_prob = jnp.einsum(
            "qhd,khd->hqk", grad_attended, head_values_ext, preferred_element_type=jnp.float32
        )
        grad_value_piece = jnp.einsum(
            "hqk,qhd->khd",
            probability.astype(jnp.bfloat16),
            grad_attended,
            preferred_element_type=jnp.float32,
        )
        row_inner = jnp.sum(grad_prob * probability, axis=-1, keepdims=True)
        grad_scores = (probability * (grad_prob - row_inner)).astype(jnp.bfloat16)
        grad_query_piece = (
            jnp.einsum("hqk,khd->qhd", grad_scores, key_piece, preferred_element_type=jnp.float32)
            * score_scale
        )
        grad_key_piece = (
            jnp.einsum("hqk,qhd->khd", grad_scores, query_piece, preferred_element_type=jnp.float32)
            * score_scale
        )
        grad_keys_ext = grad_keys_ext + grad_key_piece
        grad_values_ext = grad_values_ext + grad_value_piece
        return ((grad_keys_ext, grad_values_ext), grad_query_piece)

    zero_ext = jnp.zeros((row_count + reach_rows, HEADS, HEAD_DIM), jnp.float32)
    (grad_keys_ext, grad_values_ext), grad_query_blocks = lax.scan(
        back_block, (zero_ext, zero_ext), (starts_all, log_totals)
    )
    back_keys = from_behind(grad_keys_ext[:reach_rows].astype(jnp.bfloat16), "seq", -1).astype(
        jnp.float32
    )
    back_values = from_behind(grad_values_ext[:reach_rows].astype(jnp.bfloat16), "seq", -1).astype(
        jnp.float32
    )
    grad_query = grad_query_blocks.reshape(row_count, model_width).astype(jnp.bfloat16)
    grad_keys = (
        add_tail(grad_keys_ext[reach_rows:], back_keys)
        .reshape(row_count, model_width)
        .astype(jnp.bfloat16)
    )
    grad_values = (
        add_tail(grad_values_ext[reach_rows:], back_values)
        .reshape(row_count, model_width)
        .astype(jnp.bfloat16)
    )
    normed_cols = normed
    grad_query_matrix = weight_product(normed_cols, grad_query)
    grad_key_matrix = weight_product(normed_cols, grad_keys)
    grad_value_matrix = weight_product(normed_cols, grad_values)
    grad_normed = (
        input_product(grad_query, query_matrix)
        + input_product(grad_keys, key_matrix)
        + input_product(grad_values, value_matrix)
    )
    attention_grad_stream, grad_gain = norm_back(
        lower_stream, row_scale, norm_gain.astype(jnp.float32), grad_normed
    )
    grad_stream = grad_out + attention_grad_stream
    attention_grads = (
        grad_gain,
        grad_query_matrix,
        grad_key_matrix,
        grad_value_matrix,
        grad_output_matrix,
    )
    attention_done = settle(attention_grads)
    grad_stream, lower_grads = swiglu_back(mixed_stream, lower_full, grad_stream, lower_saved)
    lower_done = settle(lower_grads)
    grad_out = grad_stream
    normed, row_scale, extended, gate_act, conv_out = (
        mixer_normed,
        mixer_scale,
        extended,
        gate_act,
        conv_out,
    )
    norm_gain, input_matrix, gate_matrix, kernel_columns = mixer_full
    kernel = kernel_columns.T.astype(jnp.float32)
    grad_gate = (grad_out * conv_out).astype(jnp.bfloat16)
    grad_conv = grad_out * gate_act
    grad_kernel = jnp.stack(
        [
            jnp.sum(grad_conv * extended[2:], axis=0),
            jnp.sum(grad_conv * extended[1:-1], axis=0),
            jnp.sum(grad_conv * extended[:-2], axis=0),
        ],
        axis=1,
    )
    grad_extended = (
        jnp.pad(kernel[0] * grad_conv, ((2, 0), (0, 0)))
        + jnp.pad(kernel[1] * grad_conv, ((1, 1), (0, 0)))
        + jnp.pad(kernel[2] * grad_conv, ((0, 2), (0, 0)))
    )
    back_edge = from_behind(grad_extended[:2], "seq", -1)
    grad_signal = add_tail(grad_extended[2:], back_edge).astype(jnp.bfloat16)
    normed_cols = normed
    grad_input_matrix = weight_product(normed_cols, grad_signal)
    grad_gate_matrix = weight_product(normed_cols, grad_gate)
    grad_normed = input_product(grad_signal, input_matrix) + input_product(grad_gate, gate_matrix)
    mixer_grad_stream, grad_gain = norm_back(
        start_stream, row_scale, norm_gain.astype(jnp.float32), grad_normed
    )
    grad_stream = grad_out + mixer_grad_stream
    mixer_grads = (grad_gain, grad_input_matrix, grad_gate_matrix, grad_kernel)
    mixer_done = settle(mixer_grads)
    return (
        final_stream.astype(jnp.bfloat16)[None],
        grad_stream[None],
        mixer_done[0],
        mixer_done[1],
        mixer_done[2],
        mixer_done[3].T,
        lower_done[0],
        lower_done[1],
        lower_done[2],
        lower_done[3],
        attention_done[0],
        attention_done[1],
        attention_done[2],
        attention_done[3],
        attention_done[4],
        upper_done[0],
        upper_done[1],
        upper_done[2],
        upper_done[3],
    )


def solution(mesh):
    in_specs = (
        P("fsdp", "seq", None),
        P("fsdp", "seq", None),
        P("fsdp"),
        P("fsdp"),
        P("fsdp", None),
        P("fsdp", None),
        P(None, "fsdp"),
        P("fsdp"),
        P("fsdp", None),
        P("fsdp", None),
        P("fsdp", None),
        P("fsdp"),
        P("fsdp", None),
        P("fsdp", None),
        P("fsdp", None),
        P("fsdp", None),
        P("fsdp"),
        P("fsdp", None),
        P("fsdp", None),
        P("fsdp", None),
    )
    out_specs = (
        P("fsdp", "seq", None),
        P("fsdp", "seq", None),
        P("fsdp"),
        P("fsdp", None),
        P("fsdp", None),
        P(None, "fsdp"),
        P("fsdp"),
        P("fsdp", None),
        P("fsdp", None),
        P("fsdp", None),
        P("fsdp"),
        P("fsdp", None),
        P("fsdp", None),
        P("fsdp", None),
        P("fsdp", None),
        P("fsdp"),
        P("fsdp", None),
        P("fsdp", None),
        P("fsdp", None),
    )
    return jax.shard_map(body, mesh=mesh, in_specs=in_specs, out_specs=out_specs, check_vma=False)
```

profile of v0, /device:TPU:0, one launch (start us, length us, event | category | flops | bytes accessed | tf_op | source)
XLA Modules:
  0.0 1998.3 jit_solution(11742017510534794013)
XLA Ops:
  16.2 24.7 %all-gather = bf16[8,1,128]{2,1,0:T(2,128)(2,1)S(1)} all-gather(bf16[1,1,128]{2,1,0:T(2,128)(2,1)S(1)} %bitcast.171), channel_id=1, replica_groups=mesh['seq'=16,'fsdp'=8] {'fsdp'}, dimensions={0}, use_global_device_ids=true | all-gather | bytes 2304 | tf_op jit(solution)/shard_map/all_gather | solution.py:123
  41.0 18.1 all_gather.51
  59.3 7.9 all-gather.17.cloned.1.call-done
  70.6 19.0 all-gather.1
  89.6 19.0 all-gather.2
  108.6 19.0 all-gather.3
  127.7 3.3 multiply_reduce_fusion.12
  131.2 61.7 %all-gather.21.cloned.1.call-done = bf16[1024,2048]{1,0:T(8,128)(2,1)} async-done(((bf16[128,2048]{1,0:T(8,128)(2,1)}), bf16[1024,2048]{1,0:T(8,128)(2,1)}) %all-gather.21.cloned.1.call-update) | async-done | bytes 4194320 | tf_op jit(solution)/shard_map/all_gather | solution.py:123
  193.0 2.9 fusion.46
  195.9 68.6 %all-gather.23.cloned.1.call-done = bf16[1024,2048]{1,0:T(8,128)(2,1)} async-done(((bf16[128,2048]{1,0:T(8,128)(2,1)}), bf16[1024,2048]{1,0:T(8,128)(2,1)}) %all-gather.23.cloned.1.call-update) | async-done | bytes 4194320 | tf_op jit(solution)/shard_map/all_gather | solution.py:123
  264.5 4.0 multiply_convert_fusion.6
  268.5 67.5 %all-gather.25.cloned.1.call-done = bf16[2048,1024]{1,0:T(8,128)(2,1)} async-done(((bf16[256,1024]{1,0:T(8,128)(2,1)}), bf16[2048,1024]{1,0:T(8,128)(2,1)}) %all-gather.25.cloned.1.call-update) | async-done | bytes 4194320 | tf_op jit(solution)/shard_map/all_gather | solution.py:123
  336.0 3.0 multiply_reduce_fusion.11
  339.2 51.0 %all-gather.31.cloned.1.call-done = bf16[1024,1024]{1,0:T(8,128)(2,1)} async-done(((bf16[128,1024]{1,0:T(8,128)(2,1)}), bf16[1024,1024]{1,0:T(8,128)(2,1)}) %all-gather.31.cloned.1.call-update) | async-done | bytes 2097168 | tf_op jit(solution)/shard_map/all_gather | solution.py:123
  393.6 50.8 %all-gather.27.cloned.1.call-done = bf16[1024,1024]{1,0:T(8,128)(2,1)} async-done(((bf16[128,1024]{1,0:T(8,128)(2,1)}), bf16[1024,1024]{1,0:T(8,128)(2,1)}) %all-gather.27.cloned.1.call-update) | async-done | bytes 2097168 | tf_op jit(solution)/shard_map/all_gather | solution.py:123
  448.0 50.7 %all-gather.29.cloned.1.call-done = bf16[1024,1024]{1,0:T(8,128)(2,1)} async-done(((bf16[128,1024]{1,0:T(8,128)(2,1)}), bf16[1024,1024]{1,0:T(8,128)(2,1)}) %all-gather.29.cloned.1.call-update) | async-done | bytes 2097168 | tf_op jit(solution)/shard_map/all_gather | solution.py:123
  505.9 47.1 %all-gather.33.cloned.1.call-done = bf16[1024,1024]{1,0:T(8,128)(2,1)} async-done(((bf16[128,1024]{1,0:T(8,128)(2,1)}), bf16[1024,1024]{1,0:T(8,128)(2,1)}) %all-gather.33.cloned.1.call-update) | async-done | bytes 2097168 | tf_op jit(solution)/shard_map/all_gather | solution.py:123
  556.1 68.5 %all-gather.37.cloned.1.call-done = bf16[1024,2048]{1,0:T(8,128)(2,1)} async-done(((bf16[128,2048]{1,0:T(8,128)(2,1)}), bf16[1024,2048]{1,0:T(8,128)(2,1)}) %all-gather.37.cloned.1.call-update) | async-done | bytes 4194320 | tf_op jit(solution)/shard_map/all_gather | solution.py:123
  624.5 4.0 fusion.48
  628.5 67.7 %all-gather.35.cloned.1.call-done = bf16[1024,2048]{1,0:T(8,128)(2,1)} async-done(((bf16[128,2048]{1,0:T(8,128)(2,1)}), bf16[1024,2048]{1,0:T(8,128)(2,1)}) %all-gather.35.cloned.1.call-update) | async-done | bytes 4194320 | tf_op jit(solution)/shard_map/all_gather | solution.py:123
  696.2 4.0 fusion.47
  700.2 67.6 %all-gather.39.cloned.1.call-done = bf16[2048,1024]{1,0:T(8,128)(2,1)} async-done(((bf16[256,1024]{1,0:T(8,128)(2,1)}), bf16[2048,1024]{1,0:T(8,128)(2,1)}) %all-gather.39.cloned.1.call-update) | async-done | bytes 4194320 | tf_op jit(solution)/shard_map/all_gather | solution.py:123
  767.8 5.5 multiply_convert_fusion.3
  780.6 3.3 convolution_convert_fusion.12
  785.7 2.6 fusion.45
  823.8 2.8 collective-permute-done.5
  829.0 3.3 convolution_convert_fusion
  833.4 3.3 convolution_convert_fusion.1
  837.8 3.2 convolution_convert_fusion.2
  842.1 3.3 convolution_convert_fusion.3
  846.5 3.3 convolution_convert_fusion.4
  850.8 3.3 convolution_convert_fusion.5
  856.1 77.4 %reduce-scatter.26.cloned.1.call-done = bf16[128,1024]{1,0:T(8,128)(2,1)} async-done(((bf16[1024,1024]{1,0:T(8,128)(2,1)}), bf16[128,1024]{1,0:T(8,128)(2,1)}) %reduce-scatter.26.cloned.1.call-update) | async-done | bytes 262160 | tf_op jit(solution)/shard_map/reduce_scatter | solution.py:130
  933.5 77.5 %reduce-scatter.18.cloned.1.call-done = bf16[128,1024]{1,0:T(8,128)(2,1)} async-done(((bf16[1024,1024]{1,0:T(8,128)(2,1)}), bf16[128,1024]{1,0:T(8,128)(2,1)}) %reduce-scatter.18.cloned.1.call-update) | async-done | bytes 262160 | tf_op jit(solution)/shard_map/reduce_scatter | solution.py:130
  1010.9 77.5 %reduce-scatter.30.cloned.1.call-done = bf16[128,1024]{1,0:T(8,128)(2,1)} async-done(((bf16[1024,1024]{1,0:T(8,128)(2,1)}), bf16[128,1024]{1,0:T(8,128)(2,1)}) %reduce-scatter.30.cloned.1.call-update) | async-done | bytes 262160 | tf_op jit(solution)/shard_map/reduce_scatter | solution.py:130
  1088.5 77.5 %reduce-scatter.28.cloned.1.call-done = bf16[128,1024]{1,0:T(8,128)(2,1)} async-done(((bf16[1024,1024]{1,0:T(8,128)(2,1)}), bf16[128,1024]{1,0:T(8,128)(2,1)}) %reduce-scatter.28.cloned.1.call-update) | async-done | bytes 262160 | tf_op jit(solution)/shard_map/reduce_scatter | solution.py:130
  1166.0 77.4 %reduce-scatter.16.cloned.1.call-done = bf16[128,1024]{1,0:T(8,128)(2,1)} async-done(((bf16[1024,1024]{1,0:T(8,128)(2,1)}), bf16[128,1024]{1,0:T(8,128)(2,1)}) %reduce-scatter.16.cloned.1.call-update) | async-done | bytes 262160 | tf_op jit(solution)/shard_map/reduce_scatter | solution.py:130
  1243.4 87.3 %reduce-scatter.38.cloned.1.call-done = bf16[256,1024]{1,0:T(8,128)(2,1)} async-done(((bf16[2048,1024]{1,0:T(8,128)(2,1)}), bf16[256,1024]{1,0:T(8,128)(2,1)}) %reduce-scatter.38.cloned.1.call-update) | async-done | bytes 524304 | tf_op jit(solution)/shard_map/reduce_scatter | solution.py:130
  1330.7 87.6 %reduce-scatter.36.cloned.1.call-done = bf16[128,2048]{1,0:T(8,128)(2,1)} async-done(((bf16[1024,2048]{1,0:T(8,128)(2,1)}), bf16[128,2048]{1,0:T(8,128)(2,1)}) %reduce-scatter.36.cloned.1.call-update) | async-done | bytes 524304 | tf_op jit(solution)/shard_map/reduce_scatter | solution.py:130
  1418.3 87.3 %reduce-scatter.34.cloned.1.call-done = bf16[128,2048]{1,0:T(8,128)(2,1)} async-done(((bf16[1024,2048]{1,0:T(8,128)(2,1)}), bf16[128,2048]{1,0:T(8,128)(2,1)}) %reduce-scatter.34.cloned.1.call-update) | async-done | bytes 524304 | tf_op jit(solution)/shard_map/reduce_scatter | solution.py:130
  1505.6 87.8 %reduce-scatter.24.cloned.1.call-done = bf16[256,1024]{1,0:T(8,128)(2,1)} async-done(((bf16[2048,1024]{1,0:T(8,128)(2,1)}), bf16[256,1024]{1,0:T(8,128)(2,1)}) %reduce-scatter.24.cloned.1.call-update) | async-done | bytes 524304 | tf_op jit(solution)/shard_map/reduce_scatter | solution.py:130
  1593.4 87.2 %reduce-scatter.22.cloned.1.call-done = bf16[128,2048]{1,0:T(8,128)(2,1)} async-done(((bf16[1024,2048]{1,0:T(8,128)(2,1)}), bf16[128,2048]{1,0:T(8,128)(2,1)}) %reduce-scatter.22.cloned.1.call-update) | async-done | bytes 524304 | tf_op jit(solution)/shard_map/reduce_scatter | solution.py:130
  1680.6 87.5 %reduce-scatter.20.cloned.1.call-done = bf16[128,2048]{1,0:T(8,128)(2,1)} async-done(((bf16[1024,2048]{1,0:T(8,128)(2,1)}), bf16[128,2048]{1,0:T(8,128)(2,1)}) %reduce-scatter.20.cloned.1.call-update) | async-done | bytes 524304 | tf_op jit(solution)/shard_map/reduce_scatter | solution.py:130
  1770.1 3.8 fusion.5
  1776.4 21.7 %all-reduce.9 = (bf16[1024]{0:T(1024)(128)(2,1)S(1)}, bf16[1024]{0:T(1024)(128)(2,1)S(1)}, bf16[1024]{0:T(1024)(128)(2,1)S(1)}, bf16[1024]{0:T(1024)(128)(2,1)S(1)}) all-reduce(bf16[1024]{0:T(1024)(128)(2,1)S(1)} %get-tuple-element.79, bf16[1024]{0:T(1024)(128)(2,1)S(1)} %get-tuple-element.77, ...), channel_id=2, replica_groups=mesh['seq'=16,'fsdp'=8] {'fsdp'}, use_global_device_ids=true, to_apply=%region_12.13.clone | all-reduce | flops 4096 | bytes 16384
  1799.4 41.5 %reduce-scatter.40.cloned.1.call-done = bf16[128,3]{1,0:T(8,128)(2,1)} async-done(((bf16[1024,3]{1,0:T(8,128)(2,1)}), bf16[128,3]{1,0:T(8,128)(2,1)}) %reduce-scatter.40.cloned.1.call-update) | async-done | bytes 784
  1841.7 27.7 %all-reduce.7 = (bf16[128]{0:T(256)(128)(2,1)S(1)}, bf16[3,128]{1,0:T(4,128)(2,1)S(1)}, bf16[128]{0:T(256)(128)(2,1)S(1)}, bf16[128]{0:T(256)(128)(2,1)S(1)}, bf16[128]{0:T(256)(128)(2,1)S(1)}) all-reduce(bf16[128]{0:T(256)(128)(2,1)S(1)} %dynamic-slice.1, ...), channel_id=1, replica_groups=mesh['seq'=16,'fsdp'=8] {'seq'}, use_global_device_ids=true, to_apply=%region_13.14 | all-reduce | flops 896 | bytes 3584 | tf_op jit(solution)/shard_map/psum | solution.py:133
  1872.1 104.7 %all-reduce.12.cloned.1.call-done = (bf16[128,1024]{1,0:T(8,128)(2,1)}, bf16[128,1024]{1,0:T(8,128)(2,1)}, bf16[128,2048]{1,0:T(8,128)(2,1)}, bf16[128,2048]{1,0...) async-done(((bf16[128,1024]{1,0:T(8,128)(2,1)}, ...) | async-done | bytes 4718608 | tf_op jit(solution)/shard_map/psum | solution.py:133
  (307 shorter events, 105.7 us)
Async XLA Ops:
  7.2 59.9 %all-gather.17.cloned.1.call-start = ((), (), s32[]{:S(2)}) async-start(), calls=%async_computation.13 | async-start | bytes 2359296 | tf_op jit(solution)/shard_map/all_gather | solution.py:123
  7.9 119.8 %all-gather.19.cloned.1.call-start = ((), (), s32[]{:S(2)}) async-start(), calls=%async_computation.14 | async-start | bytes 2359296 | tf_op jit(solution)/shard_map/all_gather | solution.py:123
  8.7 6.7 copy-start.3
  8.7 184.3 %all-gather.21.cloned.1.call-start = ((), (), s32[]{:S(2)}) async-start(), calls=%async_computation.15 | async-start | bytes 4718592 | tf_op jit(solution)/shard_map/all_gather | solution.py:123
  9.4 6.8 copy-start.61
  9.4 31.6 %copy-start.60 = (bf16[3,128]{1,0:T(4,128)(2,1)S(1)}, bf16[3,128]{1,0:T(4,128)(2,1)}, u32[]{:S(2)}) copy-start(bf16[3,128]{1,0:T(4,128)(2,1)} %param.26) | copy-start | bytes 2308
  9.4 255.1 %all-gather.23.cloned.1.call-start = ((), (), s32[]{:S(2)}) async-start(), calls=%async_computation.16 | async-start | bytes 4718592 | tf_op jit(solution)/shard_map/all_gather | solution.py:123
  10.0 326.0 %all-gather.25.cloned.1.call-start = ((), (), s32[]{:S(2)}) async-start(), calls=%async_computation.17 | async-start | bytes 4718592 | tf_op jit(solution)/shard_map/all_gather | solution.py:123
  10.6 379.6 %all-gather.31.cloned.1.call-start = ((), (), s32[]{:S(2)}) async-start(), calls=%async_computation.20 | async-start | bytes 2359296 | tf_op jit(solution)/shard_map/all_gather | solution.py:123
  11.2 433.3 %all-gather.27.cloned.1.call-start = ((), (), s32[]{:S(2)}) async-start(), calls=%async_computation.18 | async-start | bytes 2359296 | tf_op jit(solution)/shard_map/all_gather | solution.py:123
  11.9 486.8 %all-gather.29.cloned.1.call-start = ((), (), s32[]{:S(2)}) async-start(), calls=%async_computation.19 | async-start | bytes 2359296 | tf_op jit(solution)/shard_map/all_gather | solution.py:123
  12.7 540.3 %all-gather.33.cloned.1.call-start = ((), (), s32[]{:S(2)}) async-start(), calls=%async_computation.21 | async-start | bytes 2359296 | tf_op jit(solution)/shard_map/all_gather | solution.py:123
  13.4 611.1 %all-gather.37.cloned.1.call-start = ((), (), s32[]{:S(2)}) async-start(), calls=%async_computation.23 | async-start | bytes 4718592 | tf_op jit(solution)/shard_map/all_gather | solution.py:123
  14.0 56.6 %copy-start.62 = (bf16[128]{0:T(256)(128)(2,1)S(1)}, bf16[128]{0:T(256)(128)(2,1)}, u32[]{:S(2)}) copy-start(bf16[128]{0:T(256)(128)(2,1)} %param.27) | copy-start | bytes 772
  14.0 75.6 %copy-start.63 = (bf16[128]{0:T(256)(128)(2,1)S(1)}, bf16[128]{0:T(256)(128)(2,1)}, u32[]{:S(2)}) copy-start(bf16[128]{0:T(256)(128)(2,1)} %param.31) | copy-start | bytes 772
  14.0 94.6 %copy-start.64 = (bf16[128]{0:T(256)(128)(2,1)S(1)}, bf16[128]{0:T(256)(128)(2,1)}, u32[]{:S(2)}) copy-start(bf16[128]{0:T(256)(128)(2,1)} %param.36) | copy-start | bytes 772
  14.0 682.2 %all-gather.35.cloned.1.call-start = ((), (), s32[]{:S(2)}) async-start(), calls=%async_computation.22 | async-start | bytes 4718592 | tf_op jit(solution)/shard_map/all_gather | solution.py:123
  14.8 753.0 %all-gather.39.cloned.1.call-start = ((), (), s32[]{:S(2)}) async-start(), calls=%async_computation.24 | async-start | bytes 4718592 | tf_op jit(solution)/shard_map/all_gather | solution.py:123
  15.3 840.7 %reduce-scatter.32.cloned.1.call-start = ((), (), s32[]{:S(2)}) async-start(), calls=%async_computation.33 | async-start | bytes 2359296 | tf_op jit(solution)/shard_map/reduce_scatter | solution.py:130
  69.2 58.4 %collective-permute-start = (bf16[2,1024]{1,0:T(2,128)(2,1)S(1)}, bf16[2,1024]{1,0:T(2,128)(2,1)S(1)}, u32[]{:S(2)}, u32[]{:S(2)}) collective-permute-start(bf16[2,1024]{1,0:T(2,128)(2,1)S(1)} %slice.93), channel_id=1, source_target_pairs={{0,8},{8,16},{16,24},{24,32},{32,40},{40,48},{48,56},{56,64},{64,7... | collective-permute-start | bytes 12296 | tf_op jit(solution)/shard_map/ppermute | solution.py:22
  131.2 133.3 %copy-start.14 = (bf16[128,1024]{1,0:T(8,128)(2,1)}, bf16[128,1024]{1,0:T(8,128)(2,1)S(1)}, u32[]{:S(2)}) copy-start(bf16[128,1024]{1,0:T(8,128)(2,1)S(1)} %multiply_convert_fusion.10) | copy-start | bytes 786436
  195.9 72.7 %copy-start.46 = (f32[128,2048]{1,0:T(8,128)}, f32[128,2048]{1,0:T(8,128)S(1)}, u32[]{:S(2)}) copy-start(f32[128,2048]{1,0:T(8,128)S(1)} %fusion.46) | copy-start | bytes 3145732
  268.5 70.5 %copy-start.18 = (bf16[128,2048]{1,0:T(8,128)(2,1)}, bf16[128,2048]{1,0:T(8,128)(2,1)S(1)}, u32[]{:S(2)}) copy-start(bf16[128,2048]{1,0:T(8,128)(2,1)S(1)} %get-tuple-element.119) | copy-start | bytes 1572868
  392.3 109.3 %collective-permute-start.2 = (bf16[63,1024]{1,0:T(8,128)(2,1)S(1)}, bf16[63,1024]{1,0:T(8,128)(2,1)S(1)}, u32[]{:S(2)}, u32[]{:S(2)}) collective-permute-start(bf16[63,1024]{1,0:T(8,128)(2,1)S(1)} %slice.100), channel_id=1, source_target_pairs={{0,8},{8,16},{16,24},{24,32},{32,40},{40,48},{48,56},{56,64},{64,7... | collective-permute-start | bytes 387080 | tf_op jit(solution)/shard_map/ppermute | solution.py:22
  446.5 55.4 %collective-permute-start.1 = (bf16[63,1024]{1,0:T(8,128)(2,1)S(1)}, bf16[63,1024]{1,0:T(8,128)(2,1)S(1)}, u32[]{:S(2)}, u32[]{:S(2)}) collective-permute-start(bf16[63,1024]{1,0:T(8,128)(2,1)S(1)} %slice.99), channel_id=1, source_target_pairs={{0,8},{8,16},{16,24},{24,32},{32,40},{40,48},{48,56},{56,64},{64,7... | collective-permute-start | bytes 387080 | tf_op jit(solution)/shard_map/ppermute | solution.py:22
  767.8 5.5 copy-start.1
  780.6 152.9 %reduce-scatter.26.cloned.1.call-start = ((), (), s32[]{:S(2)}) async-start(), calls=%async_computation.30 | async-start | bytes 2359296 | tf_op jit(solution)/shard_map/reduce_scatter | solution.py:130
  785.7 4.8 copy-start.28
  785.7 4.8 copy-start.35
  789.3 12.3 collective-permute-start.4
  794.5 8.4 collective-permute-start.3
  798.4 212.6 %reduce-scatter.18.cloned.1.call-start = ((), (), s32[]{:S(2)}) async-start(), calls=%async_computation.26 | async-start | bytes 2359296 | tf_op jit(solution)/shard_map/reduce_scatter | solution.py:130
  817.7 270.7 %reduce-scatter.30.cloned.1.call-start = ((), (), s32[]{:S(2)}) async-start(), calls=%async_computation.32 | async-start | bytes 2359296 | tf_op jit(solution)/shard_map/reduce_scatter | solution.py:130
  819.9 346.0 %reduce-scatter.28.cloned.1.call-start = ((), (), s32[]{:S(2)}) async-start(), calls=%async_computation.31 | async-start | bytes 2359296 | tf_op jit(solution)/shard_map/reduce_scatter | solution.py:130
  822.1 421.3 %reduce-scatter.16.cloned.1.call-start = ((), (), s32[]{:S(2)}) async-start(), calls=%async_computation.25 | async-start | bytes 2359296 | tf_op jit(solution)/shard_map/reduce_scatter | solution.py:130
  822.3 4.4 collective-permute-start.5
  828.9 501.8 %reduce-scatter.38.cloned.1.call-start = ((), (), s32[]{:S(2)}) async-start(), calls=%async_computation.36 | async-start | bytes 4718592 | tf_op jit(solution)/shard_map/reduce_scatter | solution.py:130
  832.3 586.0 %reduce-scatter.36.cloned.1.call-start = ((), (), s32[]{:S(2)}) async-start(), calls=%async_computation.35 | async-start | bytes 4718592 | tf_op jit(solution)/shard_map/reduce_scatter | solution.py:130
  836.8 668.8 %reduce-scatter.34.cloned.1.call-start = ((), (), s32[]{:S(2)}) async-start(), calls=%async_computation.34 | async-start | bytes 4718592 | tf_op jit(solution)/shard_map/reduce_scatter | solution.py:130
  841.1 752.3 %reduce-scatter.24.cloned.1.call-start = ((), (), s32[]{:S(2)}) async-start(), calls=%async_computation.29 | async-start | bytes 4718592 | tf_op jit(solution)/shard_map/reduce_scatter | solution.py:130
  845.4 835.2 %reduce-scatter.22.cloned.1.call-start = ((), (), s32[]{:S(2)}) async-start(), calls=%async_computation.28 | async-start | bytes 4718592 | tf_op jit(solution)/shard_map/reduce_scatter | solution.py:130
  849.8 918.3 %reduce-scatter.20.cloned.1.call-start = ((), (), s32[]{:S(2)}) async-start(), calls=%async_computation.27 | async-start | bytes 4718592 | tf_op jit(solution)/shard_map/reduce_scatter | solution.py:130
  854.2 986.7 %reduce-scatter.40.cloned.1.call-start = ((), (), s32[]{:S(2)}) async-start(), calls=%async_computation.37 | async-start | bytes 294912
  855.2 1121.6 %all-reduce.12.cloned.1.call-start = ((), (), s32[]{:S(2)}) async-start(), calls=%async_computation.38 | async-start | bytes 9437184 | tf_op jit(solution)/shard_map/psum | solution.py:133
  1976.8 5.5 copy-start.59
  1976.8 6.4 copy-start.58
  1976.8 7.2 copy-start.57
  1978.7 6.2 copy-start.56
  (51 other events, 109.1 us)
Sparse Core Ops, SparseCore 0:
  10.4 56.6 all-gather.16
  69.5 51.7 all-gather.18
  123.6 69.2 all-gather.20
  195.2 69.2 all-gather.22
  266.7 69.2 all-gather.24
  338.3 51.8 all-gather.30
  392.5 51.8 all-gather.26
  446.8 51.8 all-gather.28
  501.1 51.8 all-gather.32
  555.2 69.2 all-gather.36
  626.9 69.2 all-gather.34
  698.4 69.2 all-gather.38
  780.7 75.2 reduce-scatter.31
  859.6 73.8 reduce-scatter.25
  937.0 73.8 reduce-scatter.17
  1014.5 73.8 reduce-scatter.29
  1092.0 73.9 reduce-scatter.27
  1169.5 73.8 reduce-scatter.15
  1247.2 83.4 reduce-scatter.37
  1334.9 83.4 reduce-scatter.35
  1422.2 83.3 reduce-scatter.33
  1509.9 83.4 reduce-scatter.23
  1597.2 83.3 reduce-scatter.21
  1684.8 83.3 reduce-scatter.19
  1772.2 68.6 reduce-scatter.39
  1844.3 132.4 all-reduce.11
where the time goes:
time: 2000 us
  waiting for transfers between devices  1680 us (84%)
  blocking collectives  149 us (7%)
  matrix products  98.5 us (5%)
  other arithmetic  24.9 us (1%)
  local copies, waits for them, and re-layouts  20.4 us (1%)
    reduce_scatter x12, waiting for transfers between devices, settle(): lax.psum_scatter(for_sending(parts), 'fsdp', scatter_dimension=0, tiled=T...  913 us
    all_gather x12, waiting for transfers between devices, fetch(): lax.all_gather(for_sending(parts), 'fsdp', axis=0, tiled=True)  609 us
    psum x1, waiting for transfers between devices, settle(): lax.psum(for_sending(shares), 'seq')  105 us
    all_gather x5, blocking collectives, fetch(): lax.all_gather(for_sending(parts), 'fsdp', axis=0, tiled=True)  99.9 us
    unnamed x27, waiting for transfers between devices  49.2 us
  transfers between devices with their start and end apart: 32, of which 26 were waited for; matrix products, arithmetic and copies ran while one was open for 5% of the time, Pallas kernels for 0%

commit v1 on v0

v1 whole, which is shorter than its diff:
```python
import functools

import jax
import jax.numpy as jnp
from jax import lax
from jax.experimental import pallas as pl
from jax.experimental.pallas import tpu as pltpu
from jax.sharding import Mesh
from jax.sharding import PartitionSpec as P

EPSILON = 1e-05
MASKED = -1e30
AXES = ("yl", "x", "c", "yh", "z")
SIZES = (2, 4, 2, 2, 4)
F32 = jnp.float32
BF16 = jnp.bfloat16
ROWS = 128
PAIR = 256
D = 1024
HALF = 512
REACH = 64
SCALE = 64 ** (-0.5)


def at(axis):
    return lax.axis_index(axis)


def swap_core(value):
    return lax.ppermute(value, "c", [(0, 1), (1, 0)])


def hop_z(value):
    pairs = [(c * 4 + z, c * 4 + (z + 1 - 2 * c) % 4) for c in range(2) for z in range(4)]
    return lax.ppermute(value, ("c", "z"), pairs)


def cross(value):
    return lax.ppermute(value, ("yl", "yh"), [(0, 3), (3, 0), (1, 2), (2, 1)])


def swap_yl(value):
    return lax.ppermute(value, "yl", [(0, 1), (1, 0)])


def chip_shift(value, by):
    pairs = [(i, i + by) for i in range(8) if 0 <= i + by < 8]
    return lax.ppermute(value, ("yl", "x"), pairs)


def spread(value, axes, count):
    return lax.all_to_all(
        jnp.broadcast_to(value[None], (count,) + value.shape), axes, 0, 0, tiled=True
    )


def tie(values, after):
    out = lax.optimization_barrier(tuple(values) + tuple(after))
    return out[: len(values)]


def both_cores(own, other, axis=0):
    first = at("c") == 0
    return jnp.concatenate(
        [jnp.where(first, own, other), jnp.where(first, other, own)], axis=axis
    )


def gather_slabs(slabs):
    yl = at("yl")
    state = [dict(own=[s], got=[], rest=[]) for s in slabs]
    previous = ()
    for step in range(4 * len(slabs) + 1):
        wants = []
        for g, st in enumerate(state):
            k = step - 4 * g
            if 0 <= k < 3:
                wants.append((hop_z, st["own"], st["own"][k]))
            if 0 <= k < 4:
                half = lax.dynamic_index_in_dim(st["own"][k], 1 - yl, 0, keepdims=False)
                wants.append((cross, st["got"], half))
            if 1 <= k < 5:
                wants.append((swap_yl, st["rest"], st["got"][k - 1]))
        values = tie([w[2] for w in wants], previous)
        previous = [w[0](v) for w, v in zip(wants, values)]
        for w, v in zip(wants, previous):
            w[1].append(v)
    return state


def assemble_kernel(plan, count, place, *refs):
    own, got, rest = refs[0:4], refs[4:8], refs[8:12]
    outs = refs[12:-1]
    sems = refs[-1]
    copies = []

    def put(source, f, half):
        for take, out, dest in plan:
            copies.append(
                pltpu.make_async_copy(take(source), dest(outs[out], f, half), sems.at[len(copies)])
            )

    yl = place[8]
    for s in range(4):
        for half in range(2):
            put(own[s].at[half], place[s], half)
        put(got[s], place[4 + s], yl)
        put(rest[s], place[4 + s], 1 - yl)
    assert len(copies) == count
    for copy in copies:
        copy.start()
    for copy in copies:
        copy.wait()


def assemble(pieces, plan, shapes, place):
    count = 16 * len(plan)
    return pl.pallas_call(
        functools.partial(assemble_kernel, plan, count),
        out_shape=[jax.ShapeDtypeStruct(s, BF16) for s in shapes],
        in_specs=[pl.BlockSpec(memory_space=pltpu.SMEM)] + [pl.BlockSpec(memory_space=pl.ANY)] * 12,
        out_specs=[pl.BlockSpec(memory_space=pl.ANY)] * len(shapes),
        scratch_shapes=[pltpu.SemaphoreType.DMA((count,))],
        name="assemble",
    )(place, *pieces["own"], *pieces["got"], *pieces["rest"])


def rows_of(half, size=64):
    return pl.ds(half * size, size)


MIXER_PLAN = [
    (lambda s: s.at[0:64], 0, lambda o, f, h: o.at[f, rows_of(h)]),
    (lambda s: s.at[64:80], 1, lambda o, f, h: o.at[f, h]),
]
FEED_PLAN = [
    (lambda s: s.at[0], 0, lambda o, f, h: o.at[f, rows_of(h), 0:1024]),
    (lambda s: s.at[1], 0, lambda o, f, h: o.at[f, rows_of(h), 1024:2048]),
    (lambda s: s.at[2], 1, lambda o, f, h: o.at[f, rows_of(h)]),
]
HEAD_PLAN = [
    (lambda s: s.at[0], 0, lambda o, f, h: o.at[f, rows_of(h), 0:1024]),
    (lambda s: s.at[1, :, 0:512], 0, lambda o, f, h: o.at[f, rows_of(h), 1024:1536]),
    (lambda s: s.at[1, :, 512:1024], 1, lambda o, f, h: o.at[f, h]),
]


def dot(left, right, dims=((1,), (0,))):
    return lax.dot_general(left, right, (dims, ((), ())), preferred_element_type=F32)


def dot_t(left, right):
    return dot(left, right, ((1,), (1,)))


def t_dot(left, right):
    return dot(left, right, ((0,), (0,)))


def normalize(stream, gain):
    scale = lax.rsqrt(jnp.mean(stream * stream, axis=-1, keepdims=True) + EPSILON)
    return (stream * scale * gain).astype(BF16), scale


def norm_back(stream, scale, gain, upstream):
    weighted = upstream * gain
    inner = jnp.mean(weighted * stream, axis=-1, keepdims=True)
    grad = scale * (weighted - stream * scale * scale * inner)
    return grad, jnp.sum(upstream * stream * scale, axis=0)


def add_cores(partial):
    return partial + swap_core(partial.astype(BF16)).astype(F32)


def lane_mask(shape, head):
    lane = lax.broadcasted_iota(jnp.int32, shape, 1)
    return (lane // 64) == head


def window_mask(block, first):
    i = lax.broadcasted_iota(jnp.int32, (128, 192), 0)
    j = lax.broadcasted_iota(jnp.int32, (128, 192), 1)
    allowed = (j > i) & (j <= i + REACH)
    if block == 0:
        allowed = allowed & ((j >= REACH) | (first == 0))
    return allowed


def probabilities(q, k, allowed):
    scores = jnp.where(allowed, dot_t(q, k) * SCALE, MASKED)
    weights = jnp.exp(scores - jnp.max(scores, axis=-1, keepdims=True))
    return weights / jnp.sum(weights, axis=-1, keepdims=True)


def attend_kernel(first_ref, q_ref, k_ref, v_ref, o_ref):
    for block in range(2):
        allowed = window_mask(block, first_ref[0])
        rows, keys = pl.ds(block * 128, 128), pl.ds(block * 128, 192)
        for pair in range(4):
            cols = pl.ds(pair * 128, 128)
            q, k, v = q_ref[rows, cols], k_ref[keys, cols], v_ref[keys, cols]
            outs = []
            for head in range(2):
                q_head = jnp.where(lane_mask(q.shape, head), q, jnp.zeros_like(q))
                p = probabilities(q_head, k, allowed)
                outs.append(dot(p.astype(BF16), v))
            o_ref[rows, cols] = jnp.where(lane_mask(q.shape, 0), outs[0], outs[1]).astype(BF16)


def attend(first, q, k_ext, v_ext):
    return pl.pallas_call(
        attend_kernel,
        out_shape=jax.ShapeDtypeStruct((PAIR, HALF), BF16),
        in_specs=[pl.BlockSpec(memory_space=pltpu.SMEM)]
        + [pl.BlockSpec(memory_space=pltpu.VMEM)] * 3,
        out_specs=pl.BlockSpec(memory_space=pltpu.VMEM),
        name="attend",
    )(first, q, k_ext, v_ext)


def attend_back_kernel(first_ref, q_ref, k_ref, v_ref, ep_ref, eq_ref, ek_ref, ev_ref):
    for pair in range(4):
        cols = pl.ds(pair * 128, 128)
        eks, evs = [], []
        for block in range(2):
            allowed = window_mask(block, first_ref[0])
            rows, keys = pl.ds(block * 128, 128), pl.ds(block * 128, 192)
            q, k, v = q_ref[rows, cols], k_ref[keys, cols], v_ref[keys, cols]
            ep = ep_ref[rows, cols]
            eq_out, ek_out, ev_out = [], [], []
            for head in range(2):
                own = lane_mask(q.shape, head)
                p = probabilities(jnp.where(own, q, jnp.zeros_like(q)), k, allowed)
                dp = dot_t(jnp.where(own, ep, jnp.zeros_like(ep)), v)
                inner = jnp.sum(p * dp, axis=-1, keepdims=True)
                es = (p * (dp - inner)).astype(BF16)
                ev_out.append(t_dot(p.astype(BF16), ep))
                ek_out.append(t_dot(es, q))
                eq_out.append(dot(es, k))
            pick_q = lane_mask((128, 128), 0)
            pick_k = lane_mask((192, 128), 0)
            eq_ref[rows, cols] = (jnp.where(pick_q, eq_out[0], eq_out[1]) * SCALE).astype(BF16)
            eks.append(jnp.where(pick_k, ek_out[0], ek_out[1]) * SCALE)
            evs.append(jnp.where(pick_k, ev_out[0], ev_out[1]))
        for parts, ref in ((eks, ek_ref), (evs, ev_ref)):
            ref[pl.ds(0, 128), cols] = parts[0][:128]
            ref[pl.ds(128, 64), cols] = parts[0][128:] + parts[1][:64]
            ref[pl.ds(192, 128), cols] = parts[1][64:]


def attend_back(first, q, k_ext, v_ext, ep):
    return pl.pallas_call(
        attend_back_kernel,
        out_shape=[
            jax.ShapeDtypeStruct((PAIR, HALF), BF16),
            jax.ShapeDtypeStruct((PAIR + REACH, HALF), F32),
            jax.ShapeDtypeStruct((PAIR + REACH, HALF), F32),
        ],
        in_specs=[pl.BlockSpec(memory_space=pltpu.SMEM)]
        + [pl.BlockSpec(memory_space=pltpu.VMEM)] * 4,
        out_specs=[pl.BlockSpec(memory_space=pltpu.VMEM)] * 3,
        name="attend_back",
    )(first, q, k_ext, v_ext, ep)


def own_rows(value):
    return lax.dynamic_slice_in_dim(value, at("c") * ROWS, ROWS, 0)


def share_inputs(normed, hidden):
    own = own_rows(normed)
    if hidden is None:
        packed = own
    else:
        packed = jnp.concatenate([own, hidden.reshape(-1, D)], axis=0)
    got = spread(packed, "x", 4).reshape(4, -1, D)
    half = got[:, :ROWS]
    other = swap_core(half)
    all_normed = both_cores(half, other, axis=1).reshape(4 * PAIR, D)
    if hidden is None:
        return all_normed, None
    return all_normed, got[:, ROWS:].reshape(4 * PAIR, hidden.shape[1])


def share_grads(parts):
    quarters = [p.reshape(PAIR, 4, -1).transpose(1, 0, 2) for p in parts]
    packed = jnp.concatenate(quarters, axis=2)
    return lax.all_to_all(packed, "x", 0, 0, tiled=True).reshape(4 * PAIR, -1)


def settle(parts, extra=None):
    width = sum(p.shape[1] for p in parts)
    packed = jnp.concatenate([p.astype(BF16) for p in parts], axis=1)
    packed = packed.reshape(8, 2, 64, width).transpose(1, 0, 2, 3)
    if extra is not None:
        extra = jnp.pad(extra.astype(BF16), ((0, 0), (0, 16 - extra.shape[1]), (0, width - 128)))
        extra = jnp.broadcast_to(extra[None], (2,) + extra.shape)
        packed = jnp.concatenate([packed, extra], axis=2)
    rows = packed.shape[2]
    got = lax.all_to_all(packed.reshape(16, rows, width), ("yl", "yh", "z"), 0, 0, tiled=True)
    total = jnp.sum(got.astype(F32), axis=0).astype(BF16)
    return spread(total, ("yl", "x", "c"), 16).reshape(2, 4, 2, rows, width)


def body(
    inputs,
    cotangent,
    lengths,
    mixer_gain,
    mixer_input,
    mixer_gate,
    mixer_kernel,
    lower_gain,
    lower_gate,
    lower_up,
    lower_down,
    attention_gain,
    attention_query,
    attention_key,
    attention_value,
    attention_output,
    upper_gain,
    upper_gate,
    upper_up,
    upper_down,
):
    c, x, yl, yh, z = at("c"), at("x"), at("yl"), at("yh"), at("z")
    chip = yl * 4 + x
    first_chip = (chip == 0).astype(jnp.int32).reshape(1)

    def half_cols(matrix):
        return lax.dynamic_slice_in_dim(matrix, c * HALF, HALF, 1)

    def block_cols(matrix, width):
        blocks = matrix.reshape(ROWS, 8, 2, width)
        return lax.dynamic_index_in_dim(blocks, c, 2, keepdims=False).reshape(ROWS, 8 * width)

    small = jnp.concatenate(
        [
            mixer_gain[None],
            lower_gain[None],
            attention_gain[None],
            upper_gain[None],
            mixer_kernel,
            jnp.zeros((9, ROWS), BF16),
        ],
        axis=0,
    )
    small = jnp.pad(small, ((0, 0), (0, D - ROWS)))
    mixer_own = jnp.concatenate([half_cols(mixer_input), half_cols(mixer_gate)], axis=1)
    mixer_slab = jnp.concatenate(
        [mixer_own.reshape(2, 64, D), jnp.broadcast_to(small[None], (2, 16, D))], axis=1
    )

    def feed_slab(gate, up, down):
        parts = [
            block_cols(gate, ROWS),
            block_cols(up, ROWS),
            lax.dynamic_slice_in_dim(down, c * ROWS, ROWS, 0),
        ]
        return jnp.stack([p.reshape(2, 64, D) for p in parts], axis=1)

    wo = lax.dynamic_slice_in_dim(attention_output, c * 64, 64, 0)
    qk = jnp.concatenate([block_cols(attention_query, 64), block_cols(attention_key, 64)], axis=1)
    vw = jnp.concatenate(
        [
            block_cols(attention_value, 64).reshape(2, 64, HALF),
            wo.reshape(64, 2, HALF).transpose(1, 0, 2),
        ],
        axis=2,
    )
    head_slab = jnp.stack([qk.reshape(2, 64, D), vw], axis=1)

    pieces = gather_slabs(
        [
            mixer_slab,
            feed_slab(lower_gate, lower_up, lower_down),
            head_slab,
            feed_slab(upper_gate, upper_up, upper_down),
        ]
    )
    zs = [jnp.mod(z - (1 - 2 * c) * s, 4) for s in range(4)]
    place = jnp.stack([yh * 4 + v for v in zs] + [(1 - yh) * 4 + v for v in zs] + [yl]).astype(
        jnp.int32
    )
    mix_w, small_all = assemble(pieces[0], MIXER_PLAN, [(8, 128, D), (8, 2, 16, D)], place)
    mix_w = mix_w.reshape(D, D)
    small_all = small_all[:, 0, :, :ROWS].transpose(1, 0, 2).reshape(16, D).astype(F32)
    gain_m, gain_l, gain_a, gain_u = (small_all[i] for i in range(4))
    taps = lax.dynamic_slice_in_dim(small_all[4:7], c * HALF, HALF, 1)

    mine = jnp.concatenate([inputs[0], cotangent[0]], axis=1)
    two = both_cores(mine, swap_core(mine))
    start = two[:, :D].astype(F32)
    place_row = chip * PAIR + jnp.arange(PAIR, dtype=jnp.int32)
    valid = (place_row < lengths[0]).astype(F32)
    e4 = two[:, D:].astype(F32) * valid[:, None]

    halo = chip_shift(two[PAIR - 16 :, :D], 1)
    with_halo = jnp.concatenate([halo.astype(F32), start], axis=0)
    na_ext, _ = normalize(with_halo, gain_m)
    na = na_ext[16:]
    scale_a = lax.rsqrt(jnp.mean(start * start, axis=-1, keepdims=True) + EPSILON)
    both = dot(na_ext, mix_w)
    signal = both[:, :HALF].astype(BF16).astype(F32)
    gate = both[16:, HALF:]
    shifted = [signal[16:], signal[15:-1], signal[14:-2]]
    conv = sum(taps[m] * shifted[m] for m in range(3))
    mixed = conv * gate
    h1 = start + both_cores(mixed, swap_core(mixed.astype(BF16)).astype(F32), axis=1)

    def feed(stream, gain, weights):
        w_in, w_out = weights
        normed, scale = normalize(stream, gain)
        act = dot(normed, w_in)
        hidden = (jax.nn.silu(act[:, :D]) * act[:, D:]).astype(BF16)
        return normed, scale, act, hidden, dot(hidden, w_out)

    def feed_weights(k):
        w_in, w_out = assemble(pieces[k], FEED_PLAN, [(8, 128, 2 * D), (8, 128, D)], place)
        return w_in.reshape(D, 2 * D), w_out.reshape(D, D)

    lower_w = feed_weights(1)
    nb, scale_b, act_l, ha, part = feed(h1, gain_l, lower_w)
    h2 = h1 + add_cores(part)

    qkv_w, out_w = assemble(pieces[2], HEAD_PLAN, [(8, 128, 3 * HALF), (8, 2, 64, HALF)], place)
    qkv_w = qkv_w.reshape(D, 3 * HALF)
    out_w = out_w.transpose(0, 2, 1, 3).reshape(HALF, D)
    nc, scale_c = normalize(h2, gain_a)
    qkv = dot(nc, qkv_w).astype(BF16)
    q = qkv[:, :HALF]
    edge = chip_shift(qkv[PAIR - REACH :, HALF:], 1)
    kv_ext = jnp.concatenate([edge, qkv[:, HALF:]], axis=0)
    k_ext, v_ext = kv_ext[:, :HALF], kv_ext[:, HALF:]
    o = attend(first_chip, q, k_ext, v_ext)
    h3 = h2 + add_cores(dot(o, out_w))

    upper_w = feed_weights(3)
    nd, scale_d, act_u, hb, part = feed(h3, gain_u, upper_w)
    other_part = lax.dynamic_slice_in_dim(part, (1 - c) * ROWS, ROWS, 0).astype(BF16)
    outputs = own_rows(h3) + own_rows(part) + swap_core(other_part).astype(F32)

    nd_all, hb_all = share_inputs(nd, hb)
    nb_all, ha_all = share_inputs(nb, ha)
    nc_all, o_all = share_inputs(nc, o)
    na_all, _ = share_inputs(na, None)

    def feed_back(stream, scale, gain, weights, act, grad_out, n_all, h_all):
        w_in, w_out = weights
        branch = grad_out.astype(BF16)
        grad_hidden = dot_t(branch, w_out)
        gate_act, up_act = act[:, :D], act[:, D:]
        sig = jax.nn.sigmoid(gate_act)
        grad_gate = (grad_hidden * up_act * sig * (1.0 + gate_act * (1.0 - sig))).astype(BF16)
        grad_up = (grad_hidden * gate_act * sig).astype(BF16)
        both_grads = jnp.concatenate([grad_gate, grad_up], axis=1)
        grad_normed = add_cores(dot_t(both_grads, w_in))
        grad_stream, grad_gain = norm_back(stream, scale, gain, grad_normed)
        shared = share_grads([grad_gate, grad_up, branch])
        done = settle([t_dot(n_all, shared[:, : D // 2]), t_dot(h_all, shared[:, D // 2 :])])
        return grad_out + grad_stream, grad_gain, done

    e3, gain_grad_u, done_u = feed_back(h3, scale_d, gain_u, upper_w, act_u, e4, nd_all, hb_all)

    eo = e3.astype(BF16)
    ep = dot_t(eo, out_w).astype(BF16)
    eq, ek_ext, ev_ext = attend_back(first_chip, q, k_ext, v_ext, ep)
    ekv_edge = jnp.concatenate([ek_ext[:REACH], ev_ext[:REACH]], axis=1).astype(BF16)
    back = chip_shift(ekv_edge, -1).astype(F32)
    ekv = jnp.concatenate([ek_ext[REACH:], ev_ext[REACH:]], axis=1)
    ekv = jnp.concatenate([ekv[: PAIR - REACH], ekv[PAIR - REACH :] + back], axis=0).astype(BF16)
    eqkv = jnp.concatenate([eq, ekv], axis=1)
    grad_nc = add_cores(dot_t(eqkv, qkv_w))
    grad_stream, gain_grad_a = norm_back(h2, scale_c, gain_a, grad_nc)
    e2 = e3 + grad_stream
    shared = share_grads([eq, ekv[:, :HALF], ekv[:, HALF:], eo])
    out_grad = t_dot(o_all, shared[:, 384:])
    out_grad = out_grad.reshape(8, 64, 2, 128).transpose(0, 2, 1, 3).reshape(D, 128)
    done_a = settle([t_dot(nc_all, shared[:, :384]), out_grad])

    e1, gain_grad_l, done_l = feed_back(h1, scale_b, gain_l, lower_w, act_l, e2, nb_all, ha_all)

    e1_own = lax.dynamic_slice_in_dim(e1, c * HALF, HALF, 1)
    egate = (e1_own * conv).astype(BF16)
    ec = e1_own * gate
    tap_grads = jnp.stack([jnp.sum(ec * shifted[m], axis=0) for m in range(3)])
    ec_next = chip_shift(ec[:8], -1)
    ec_ext = jnp.concatenate([ec, ec_next], axis=0)
    esig = sum(taps[m] * ec_ext[m : m + PAIR] for m in range(3)).astype(BF16)
    emix = jnp.concatenate([esig, egate], axis=1)
    grad_na = dot_t(emix, mix_w)
    other_na = lax.dynamic_slice_in_dim(grad_na, (1 - c) * ROWS, ROWS, 0).astype(BF16)
    grad_na = own_rows(grad_na) + swap_core(other_na).astype(F32)
    grad_start, gain_grad_m = norm_back(own_rows(start), own_rows(scale_a), gain_m, grad_na)
    input_grad = own_rows(e1) + grad_start
    shared = share_grads([esig, egate])
    once = (c == 0).astype(F32)
    wide_taps = lax.dynamic_update_slice(jnp.zeros((3, D), F32), tap_grads, (0, c * HALF))
    gains = jnp.stack([gain_grad_m, gain_grad_l * once, gain_grad_a * once, gain_grad_u * once])
    extra = jnp.concatenate([gains, wide_taps], axis=0).reshape(7, 8, ROWS).transpose(1, 0, 2)
    done_m = settle([t_dot(na_all, shared)], extra)

    def in_cols(part, width):
        part = part.reshape(2, 4, 2, 64, 2, width).transpose(0, 3, 1, 4, 2, 5)
        return part.reshape(ROWS, 16 * width).astype(F32)

    def feed_grads(done):
        down = done[..., 512:].transpose(2, 0, 3, 1, 4).reshape(2 * ROWS, D).astype(F32)
        return in_cols(done[..., :256], 128), in_cols(done[..., 256:512], 128), down

    def head_grads(done):
        out = done[..., 384:].transpose(2, 3, 1, 0, 4).reshape(ROWS, D).astype(F32)
        return [in_cols(done[..., 128 * i : 128 * i + 128], 64) for i in range(3)] + [out]

    def half_grads(part):
        return part.transpose(0, 3, 2, 1, 4).reshape(ROWS, D).astype(F32)

    tail = jnp.sum(done_m[0, :, :, 64:, :ROWS].astype(F32), axis=(0, 1))
    lower_grads, upper_grads, heads = feed_grads(done_l), feed_grads(done_u), head_grads(done_a)
    return (
        outputs.astype(BF16)[None],
        input_grad[None],
        tail[0],
        half_grads(done_m[:, :, :, :64, :128]),
        half_grads(done_m[:, :, :, :64, 128:]),
        tail[4:7],
        tail[1],
        *lower_grads,
        tail[2],
        *heads,
        tail[3],
        *upper_grads,
    )


def solution(mesh):
    fine = Mesh(mesh.devices.reshape(SIZES), AXES)
    rows = ("yh", "z")
    slots = P(rows, ("yl", "x", "c"), None)
    vector, matrix, columns = P(rows), P(rows, None), P(None, rows)
    weights = (
        (vector, matrix, matrix, columns)
        + (vector, matrix, matrix, matrix)
        + (vector, matrix, matrix, matrix, matrix)
        + (vector, matrix, matrix, matrix)
    )
    return jax.shard_map(
        body,
        mesh=fine,
        in_specs=(slots, slots, vector) + weights,
        out_specs=(slots, slots) + weights,
        check_vma=False,
    )
```

time: 2000 us -> 1300 us (0.65)
  waiting for transfers between devices: 1680 us -> 239 us
  Pallas kernels: 0 us -> 614 us
  local copies, waits for them, and re-layouts: 20.4 us -> 177 us
  blocking collectives: 149 us -> 0 us
  starting transfers between devices: 9.55 us -> 135 us
  matrix products: 98.5 us -> 45.9 us
  other arithmetic: 24.9 us -> 73.9 us
    reduce_scatter x12 -> x0, waiting for transfers between devices: 913 us -> none  [settle(): lax.psum_scatter(for_sending(parts), 'fsdp', scatter_dimension=0, tiled=T...]
    pallas_call x0 -> x6, Pallas kernels: none -> 614 us  [the longest x4 596 us: assemble(): pl.pallas_call(functools.partial(assemble_kernel, plan, count), out_shape...]
    all_gather x12 -> x0, waiting for transfers between devices: 609 us -> none  [fetch(): lax.all_gather(for_sending(parts), 'fsdp', axis=0, tiled=True)]
    all_to_all x0 -> x16, waiting for transfers between devices: none -> 128 us  [the longest x8 76.7 us: spread(): lax.all_to_all(jnp.broadcast_to(value[None], (count,) + value.shape), axe...]
    ppermute x6 -> x61, waiting for transfers between devices: 2.86 us -> 111 us  [the longest x12 34.4 us: hop_z(): return lax.ppermute(value, ('c', 'z'), pairs)]
    psum x1 -> x0, waiting for transfers between devices: 105 us -> none  [settle(): lax.psum(for_sending(shares), 'seq')]
    all_gather x5 -> x0, blocking collectives: 99.9 us -> none  [fetch(): lax.all_gather(for_sending(parts), 'fsdp', axis=0, tiled=True)]
    all_to_all x0 -> x16, starting transfers between devices: none -> 76.9 us  [the longest x8 35.1 us: spread(): lax.all_to_all(jnp.broadcast_to(value[None], (count,) + value.shape), axe...]
  transfers between devices with their start and end apart: 32 -> 77, of which waited for: 26 -> 41; matrix products, arithmetic and copies ran while one was open for 5% -> 21% of each run, Pallas kernels for 0% -> 48%
where the time goes in v1:
time: 1300 us; the launch traced here: 1290 us
  Pallas kernels  614 us (47%)
  waiting for transfers between devices  239 us (18%)
  local copies, waits for them, and re-layouts  177 us (14%)
  starting transfers between devices  135 us (10%)
  other arithmetic  73.9 us (6%)
  matrix products  45.9 us (4%)
    pallas_call x4, Pallas kernels, assemble(): pl.pallas_call(functools.partial(assemble_kernel, plan, count), out_shape...  596 us
    all_to_all x8, waiting for transfers between devices, spread(): lax.all_to_all(jnp.broadcast_to(value[None], (count,) + value.shape), axe...  76.7 us
    dot_general x21, matrix products, dot(): lax.dot_general(left, right, (dims, ((), ())), preferred_element_type=F32)  45.9 us
    convert_element_type x21, local copies, waits for them, and re-layouts, in_cols(): return part.reshape(ROWS, 16 * width).astype(F32)  39 us
    all_to_all x8, starting transfers between devices, spread(): lax.all_to_all(jnp.broadcast_to(value[None], (count,) + value.shape), axe...  35.1 us
    ppermute x12, waiting for transfers between devices, hop_z(): return lax.ppermute(value, ('c', 'z'), pairs)  34.4 us
    ppermute x16, waiting for transfers between devices, cross(): return lax.ppermute(value, ('yl', 'yh'), [(0, 3), (3, 0), (1, 2), (2, 1)])  30.1 us
    ppermute x16, starting transfers between devices, cross(): return lax.ppermute(value, ('yl', 'yh'), [(0, 3), (3, 0), (1, 2), (2, 1)])  29 us
  transfers between devices with their start and end apart: 77, of which 41 were waited for; matrix products, arithmetic and copies ran while one was open for 21% of the time, Pallas kernels for 48%

profile of v1, /device:TPU:0, one launch (start us, length us, event | category | flops | bytes accessed | tf_op | source)
XLA Modules:
  0.0 1288.5 jit_solution(10590617159877591286)
XLA Ops:
  25.7 3.8 collective-permute-done.4.refs_5_
  33.4 4.5 collective-permute-done.6.refs_3_
  67.2 81.5 %assemble.4 = (bf16[8,128,1024]{2,1,0:T(8,128)(2,1)}, bf16[8,2,16,1024]{3,2,1,0:T(8,128)(2,1)}) custom-call(s32[9]{0:T(128)} %stack.67.place, bf16[2,80,1024]{2,1,0:T(8,128)(2,1)} %copy-done.49, bf16[2,80,1024]{2,1,0:T(8,128)(2,1)} %copy-done.64, bf16[2,80,1024]{2,1,0:T(8,128)(2,1)} %copy-done.65, bf16[2,80,1024]{2,1,0:T(8,128)(2,1)} %copy-done.66, ...), custom_call_target="tpu_custom_call" | custom-call | tf_op jit(solution)/shard_map/assemble/pallas_call | solution.py:118
  152.1 6.6 collective-permute-done.17.refs_5_
  163.2 10.3 collective-permute-done.19.refs_3_
  189.7 4.8 collective-permute-done.26.refs_1_
  201.9 192.8 %assemble.5 = (bf16[8,128,2048]{2,1,0:T(8,128)(2,1)}, bf16[8,128,1024]{2,1,0:T(8,128)(2,1)}) custom-call(s32[9]{0:T(128)} %stack.67.place, bf16[2,3,64,1024]{3,2,1,0:T(8,128)(2,1)} %copy-done.12, bf16[2,3,64,1024]{3,2,1,0:T(8,128)(2,1)} %collective-permute-done.14.refs_1_, bf16[2,3,64,1024]{3,2,1,0:T(8,128)(2,1)} %copy-done.46, ...), custom_call_target="tpu_custom_call" | custom-call | tf_op jit(solution)/shard_map/assemble/pallas_call | solution.py:118
  402.6 3.8 collective-permute-done.31.refs_3_
  422.7 7.5 collective-permute-done.39.refs_1_
  433.1 129.3 %assemble.6 = (bf16[8,128,1536]{2,1,0:T(8,128)(2,1)}, bf16[8,2,64,512]{3,2,1,0:T(8,128)(2,1)}) custom-call(s32[9]{0:T(128)} %stack.67.place, bf16[2,2,64,1024]{3,2,1,0:T(8,128)(2,1)} %copy-done.26, bf16[2,2,64,1024]{3,2,1,0:T(8,128)(2,1)} %copy-done.50, bf16[2,2,64,1024]{3,2,1,0:T(8,128)(2,1)} %collective-permute-done.28.refs_2_, ...), custom_call_target="tpu_custom_call" | custom-call | tf_op jit(solution)/shard_map/assemble/pallas_call | solution.py:118
  578.7 7.2 attend.1
  594.1 8.1 collective-permute-done.45.refs_6_
  608.1 4.3 all-to-all-start
  617.1 8.6 collective-permute-done.49.refs_11_
  625.7 192.8 %assemble.7 = (bf16[8,128,2048]{2,1,0:T(8,128)(2,1)}, bf16[8,128,1024]{2,1,0:T(8,128)(2,1)}) custom-call(s32[9]{0:T(128)} %stack.67.place, bf16[2,3,64,1024]{3,2,1,0:T(8,128)(2,1)} %pad_maximum_fusion.11.refs_0_, bf16[2,3,64,1024]{3,2,1,0:T(8,128)(2,1)} %collective-permute-done.39.refs_1_, bf16[2,3,64,1024]{3,2,1,0:T(8,128)(2,1)} %collective-permute-done.41.refs_2_, ...), custom_call_target="tpu_custom_call" | custom-call | tf_op jit(solution)/shard_map/assemble/pallas_call | solution.py:118
  818.5 3.7 fusion.73
  834.1 4.8 all-to-all-start.4
  846.0 10.5 attend_back.1
  864.5 14.4 %collective-permute-done.52 = bf16[64,1024]{1,0:T(8,128)(2,1)} collective-permute-done((bf16[64,1024]{1,0:T(8,128)(2,1)}, bf16[64,1024]{1,0:T(8,128)(2,1)}, u32[]{:S(2)}, u32[]{:S(2)}) %collective-permute-start.52) | collective-permute-done | bytes 131104 | tf_op jit(solution)/shard_map/ppermute | solution.py:48
  888.1 4.5 all-to-all-start.8
  902.6 17.3 %all-to-all-done.8 = bf16[4,256,1024]{1,2,0:T(8,128)(2,1)} async-done(((bf16[4,256,1024]{1,2,0:T(8,128)(2,1)}), bf16[4,256,1024]{1,2,0:T(8,128)(2,1)}, u32[]{:S(2)}, u32[]{:S(2)}) %all-to-all-start.8) | async-done | bytes 2097184 | tf_op jit(solution)/shard_map/all_to_all | solution.py:52
  920.0 4.8 all-to-all-start.13
  929.6 16.0 %all-to-all-done.13 = bf16[4,256,768]{2,1,0:T(8,128)(2,1)} async-done(((bf16[4,256,768]{2,1,0:T(8,128)(2,1)}), bf16[4,256,768]{2,1,0:T(8,128)(2,1)}, u32[]{:S(2)}, u32[]{:S(2)}) %all-to-all-start.13) | async-done | bytes 1572896 | tf_op jit(solution)/shard_map/all_to_all | solution.py:289
  945.7 4.3 all-to-all-start.9
  955.0 10.9 collective-permute-done.55
  967.2 3.8 all-to-all-start.1
  971.5 7.6 all-to-all-done.1
  981.1 4.7 all-to-all-start.12
  994.4 26.1 %all-to-all-done.12 = bf16[4,384,1024]{1,2,0:T(8,128)(2,1)} async-done(((bf16[4,384,1024]{1,2,0:T(8,128)(2,1)}), bf16[4,384,1024]{1,2,0:T(8,128)(2,1)}, u32[]{:S(2)}, u32[]{:S(2)}) %all-to-all-start.12) | async-done | bytes 3145760 | tf_op jit(solution)/shard_map/all_to_all | solution.py:52
  1020.4 5.6 all-to-all-start.2
  1029.8 6.6 all-to-all-done.2
  1036.4 4.3 all-to-all-start.5
  1043.8 4.0 copy.146
  1053.3 4.0 copy.142
  1061.1 4.9 all-to-all-start.3
  1078.3 4.4 all-to-all-start.6
  1087.8 4.0 copy.173
  1091.8 5.0 broadcast_select_fusion.1
  1108.7 4.0 copy.153
  1121.1 7.3 all-to-all-start.10
  1132.7 4.0 copy.169
  1146.4 7.2 all-to-all-start.14
  1153.8 20.6 %all-to-all-done.14 = bf16[16,64,768]{2,1,0:T(8,128)(2,1)} async-done(((bf16[16,64,768]{2,1,0:T(8,128)(2,1)}), bf16[16,64,768]{2,1,0:T(8,128)(2,1)}, u32[]{:S(2)}, u32[]{:S(2)}) %all-to-all-start.14) | async-done | bytes 1572896 | tf_op jit(solution)/shard_map/all_to_all | solution.py:301
  1175.8 3.7 all-to-all-start.7
  1180.9 20.6 %all-to-all-done.7 = bf16[16,64,768]{2,1,0:T(8,128)(2,1)S(1)} async-done(((bf16[16,64,768]{2,1,0:T(8,128)(2,1)}), bf16[16,64,768]{2,1,0:T(8,128)(2,1)S(1)}, u32[]{:S(2)}, u32[]{:S(2)}) %all-to-all-start.7) | async-done | bytes 1572896 | tf_op jit(solution)/shard_map/all_to_all | solution.py:52
  1202.7 4.3 all-to-all-start.11
  1213.6 10.0 all-to-all-done.11
  1224.9 3.9 all-to-all-start.15
  (583 shorter events, 357.2 us)
Async XLA Ops:
  4.4 12.9 %collective-permute-start.2 = (bf16[80,1024]{1,0:T(8,128)(2,1)}, bf16[80,1024]{1,0:T(8,128)(2,1)S(1)}, u32[]{:S(2)}, u32[]{:S(2)}) collective-permute-start(bf16[80,1024]{1,0:T(8,128)(2,1)} %fusion.53), channel_id=1, source_target_pairs={{0,68},{68,0},{4,64},{64,4},{1,69},{69,1},{5,65},{65,5},{2,70},{70... | collective-permute-start | bytes 491528 | tf_op jit(solution)/shard_map/ppermute | solution.py:39
  10.3 43.9 %collective-permute-start = (bf16[128,2048]{1,0:T(8,128)(2,1)}, bf16[128,2048]{1,0:T(8,128)(2,1)}, u32[]{:S(2)}, u32[]{:S(2)}) collective-permute-start(bf16[128,2048]{1,0:T(8,128)(2,1)} %pad_maximum_fusion.17), channel_id=1, source_target_pairs={{0,8},{8,0},{1,9},{9,1},{2,10},{10,2},{3,11},{11,3},{4,12},{12,4},... | collective-permute-start | bytes 1572872 | tf_op jit(solution)/shard_map/ppermute | solution.py:30
  45.2 15.4 %collective-permute-start.14 = (bf16[2,3,64,1024]{3,2,1,0:T(8,128)(2,1)S(1)}, bf16[2,3,64,1024]{3,2,1,0:T(8,128)(2,1)}, u32[]{:S(2)}, u32[]{:S(2)}) collective-permute-start(bf16[2,3,64,1024]{3,2,1,0:T(8,128)(2,1)S(1)} %pad_maximum_fusion.10.refs_0_), channel_id=1, source_target_pairs={{0,1},{1,2},{2,3},{3,0},{8,11},{9,8},{10,9},{11,10},{4,5},{5,6},{6... | collective-permute-start | bytes 2359304 | tf_op jit(solution)/shard_map/ppermute | solution.py:35
  52.3 12.9 %collective-permute-start.15 = (bf16[3,64,1024]{2,1,0:T(8,128)(2,1)}, bf16[3,64,1024]{2,1,0:T(8,128)(2,1)}, u32[]{:S(2)}, u32[]{:S(2)}) collective-permute-start(bf16[3,64,1024]{2,1,0:T(8,128)(2,1)} %dynamic-slice_bitcast_fusion.7), channel_id=1, source_target_pairs={{0,68},{68,0},{4,64},{64,4},{1,69},{69,1},{5,65},{65,5},{2,70},{70... | collective-permute-start | bytes 1179656 | tf_op jit(solution)/shard_map/ppermute | solution.py:39
  65.2 86.9 %collective-permute-start.16 = (bf16[2,3,64,1024]{3,2,1,0:T(8,128)(2,1)}, bf16[2,3,64,1024]{3,2,1,0:T(8,128)(2,1)S(1)}, u32[]{:S(2)}, u32[]{:S(2)}) collective-permute-start(bf16[2,3,64,1024]{3,2,1,0:T(8,128)(2,1)} %collective-permute-done.14.refs_1_), channel_id=1, source_target_pairs={{0,1},{1,2},{2,3},{3,0},{8,11},{9,8},{10,9},{11,10},{4,5},{5,6},{6... | collective-permute-start | bytes 2359304 | tf_op jit(solution)/shard_map/ppermute | solution.py:35
  160.3 13.2 %collective-permute-start.19 = (bf16[2,3,64,1024]{3,2,1,0:T(8,128)(2,1)S(1)}, bf16[2,3,64,1024]{3,2,1,0:T(8,128)(2,1)S(1)}, u32[]{:S(2)}, u32[]{:S(2)}) collective-permute-start(bf16[2,3,64,1024]{3,2,1,0:T(8,128)(2,1)S(1)} %collective-permute-done.16.refs_2_), channel_id=1, source_target_pairs={{0,1},{1,2},{2,3},{3,0},{8,11},{9,8},{10,9},{11,10},{4,5},{5,6},{6... | collective-permute-start | bytes 2359304 | tf_op jit(solution)/shard_map/ppermute | solution.py:35
  162.0 12.2 collective-permute-start.20
  163.1 11.1 collective-permute-start.21
  177.0 11.5 collective-permute-start.13
  196.4 198.3 %collective-permute-start.28 = (bf16[2,2,64,1024]{3,2,1,0:T(8,128)(2,1)S(1)}, bf16[2,2,64,1024]{3,2,1,0:T(8,128)(2,1)}, u32[]{:S(2)}, u32[]{:S(2)}) collective-permute-start(bf16[2,2,64,1024]{3,2,1,0:T(8,128)(2,1)S(1)} %collective-permute-done.26.refs_1_), channel_id=1, source_target_pairs={{0,1},{1,2},{2,3},{3,0},{8,11},{9,8},{10,9},{11,10},{4,5},{5,6},{6... | collective-permute-start | bytes 1572872 | tf_op jit(solution)/shard_map/ppermute | solution.py:35
  198.8 196.9 %collective-permute-start.29 = (bf16[2,64,1024]{2,1,0:T(8,128)(2,1)}, bf16[2,64,1024]{2,1,0:T(8,128)(2,1)}, u32[]{:S(2)}, u32[]{:S(2)}) collective-permute-start(bf16[2,64,1024]{2,1,0:T(8,128)(2,1)} %dynamic-slice_bitcast_fusion.10), channel_id=1, source_target_pairs={{0,68},{68,0},{4,64},{64,4},{1,69},{69,1},{5,65},{65,5},{2,70},{70... | collective-permute-start | bytes 786440 | tf_op jit(solution)/shard_map/ppermute | solution.py:39
  200.6 195.2 %collective-permute-start.30 = (bf16[2,64,1024]{2,1,0:T(8,128)(2,1)S(1)}, bf16[2,64,1024]{2,1,0:T(8,128)(2,1)}, u32[]{:S(2)}, u32[]{:S(2)}) collective-permute-start(bf16[2,64,1024]{2,1,0:T(8,128)(2,1)S(1)} %collective-permute-done.27.refs_4_), channel_id=1, source_target_pairs={{0,64},{64,0},{1,65},{65,1},{2,66},{66,2},{3,67},{67,3},{4,68},{68... | collective-permute-start | bytes 786440 | tf_op jit(solution)/shard_map/ppermute | solution.py:43
  411.4 10.9 collective-permute-start.25
  416.7 13.5 %collective-permute-start.39 = (bf16[2,3,64,1024]{3,2,1,0:T(8,128)(2,1)}, bf16[2,3,64,1024]{3,2,1,0:T(8,128)(2,1)}, u32[]{:S(2)}, u32[]{:S(2)}) collective-permute-start(bf16[2,3,64,1024]{3,2,1,0:T(8,128)(2,1)} %pad_maximum_fusion.11.refs_0_), channel_id=1, source_target_pairs={{0,1},{1,2},{2,3},{3,0},{8,11},{9,8},{10,9},{11,10},{4,5},{5,6},{6... | collective-permute-start | bytes 2359304 | tf_op jit(solution)/shard_map/ppermute | solution.py:35
  418.0 14.0 %collective-permute-start.36 = (bf16[2,64,1024]{2,1,0:T(8,128)(2,1)S(1)}, bf16[2,64,1024]{2,1,0:T(8,128)(2,1)S(1)}, u32[]{:S(2)}, u32[]{:S(2)}) collective-permute-start(bf16[2,64,1024]{2,1,0:T(8,128)(2,1)S(1)} %collective-permute-done.34.refs_7_), channel_id=1, source_target_pairs={{0,64},{64,0},{1,65},{65,1},{2,66},{66,2},{3,67},{67,3},{4,68},{68... | collective-permute-start | bytes 786440 | tf_op jit(solution)/shard_map/ppermute | solution.py:43
  420.2 11.8 collective-permute-start.40
  432.0 139.5 %collective-permute-start.41 = (bf16[2,3,64,1024]{3,2,1,0:T(8,128)(2,1)}, bf16[2,3,64,1024]{3,2,1,0:T(8,128)(2,1)}, u32[]{:S(2)}, u32[]{:S(2)}) collective-permute-start(bf16[2,3,64,1024]{3,2,1,0:T(8,128)(2,1)} %collective-permute-done.39.refs_1_), channel_id=1, source_target_pairs={{0,1},{1,2},{2,3},{3,0},{8,11},{9,8},{10,9},{11,10},{4,5},{5,6},{6... | collective-permute-start | bytes 2359304 | tf_op jit(solution)/shard_map/ppermute | solution.py:35
  562.4 10.9 collective-permute-start.42
  573.3 19.0 %collective-permute-start.44 = (bf16[2,3,64,1024]{3,2,1,0:T(8,128)(2,1)}, bf16[2,3,64,1024]{3,2,1,0:T(8,128)(2,1)}, u32[]{:S(2)}, u32[]{:S(2)}) collective-permute-start(bf16[2,3,64,1024]{3,2,1,0:T(8,128)(2,1)} %collective-permute-done.41.refs_2_), channel_id=1, source_target_pairs={{0,1},{1,2},{2,3},{3,0},{8,11},{9,8},{10,9},{11,10},{4,5},{5,6},{6... | collective-permute-start | bytes 2359304 | tf_op jit(solution)/shard_map/ppermute | solution.py:35
  588.9 23.5 %collective-permute-start.38 = (bf16[256,1024]{1,0:T(8,128)(2,1)}, bf16[256,1024]{1,0:T(8,128)(2,1)}, u32[]{:S(2)}, u32[]{:S(2)}) collective-permute-start(bf16[256,1024]{1,0:T(8,128)(2,1)} %get-tuple-element.203), channel_id=1, source_target_pairs={{0,8},{8,0},{1,9},{9,1},{2,10},{10,2},{3,11},{11,3},{4,12},{12,4},... | collective-permute-start | bytes 1572872 | tf_op jit(solution)/shard_map/ppermute | solution.py:30
  588.9 13.3 %collective-permute-start.45 = (bf16[3,64,1024]{2,1,0:T(8,128)(2,1)S(1)}, bf16[3,64,1024]{2,1,0:T(8,128)(2,1)}, u32[]{:S(2)}, u32[]{:S(2)}) collective-permute-start(bf16[3,64,1024]{2,1,0:T(8,128)(2,1)S(1)} %copy-done.84), channel_id=1, source_target_pairs={{0,68},{68,0},{4,64},{64,4},{1,69},{69,1},{5,65},{65,5},{2,70},{70... | collective-permute-start | bytes 1179656 | tf_op jit(solution)/shard_map/ppermute | solution.py:39
  592.3 11.4 collective-permute-start.46
  603.7 11.9 collective-permute-start.47
  605.1 10.7 collective-permute-start.48
  608.1 223.0 %all-to-all-start = ((bf16[4,128,1024]{1,2,0:T(8,128)(2,1)}), bf16[4,128,1024]{1,2,0:T(8,128)(2,1)}, u32[]{:S(2)}, u32[]{:S(2)}) async-start(bf16[4,128,1024]{1,2,0:T(8,128)(2,1)} %broadcast_in_dim.44), calls=%async_computation | async-start | bytes 2097152 | tf_op jit(solution)/shard_map/all_to_all | solution.py:52
  827.0 12.0 collective-permute-start.51
  834.1 52.6 %all-to-all-start.4 = ((bf16[4,384,1024]{1,2,0:T(8,128)(2,1)}), bf16[4,384,1024]{1,2,0:T(8,128)(2,1)}, u32[]{:S(2)}, u32[]{:S(2)}) async-start(bf16[4,384,1024]{1,2,0:T(8,128)(2,1)} %broadcast_in_dim.48), calls=%async_computation.4 | async-start | bytes 6291456 | tf_op jit(solution)/shard_map/all_to_all | solution.py:52
  859.0 19.8 %collective-permute-start.52 = (bf16[64,1024]{1,0:T(8,128)(2,1)}, bf16[64,1024]{1,0:T(8,128)(2,1)}, u32[]{:S(2)}, u32[]{:S(2)}) collective-permute-start(bf16[64,1024]{1,0:T(8,128)(2,1)} %pad_maximum_fusion.26), channel_id=1, source_target_pairs={{16,0},{32,16},{48,32},{64,48},{80,64},{96,80},{112,96},{17,1},{33... | collective-permute-start | bytes 393224 | tf_op jit(solution)/shard_map/ppermute | solution.py:48
  888.1 31.8 %all-to-all-start.8 = ((bf16[4,256,1024]{1,2,0:T(8,128)(2,1)}), bf16[4,256,1024]{1,2,0:T(8,128)(2,1)}, u32[]{:S(2)}, u32[]{:S(2)}) async-start(bf16[4,256,1024]{1,2,0:T(8,128)(2,1)} %broadcast_in_dim.50), calls=%async_computation.8 | async-start | bytes 4194304 | tf_op jit(solution)/shard_map/all_to_all | solution.py:52
  902.1 26.2 %collective-permute-start.54 = (bf16[256,1024]{1,0:T(8,128)(2,1)}, bf16[256,1024]{1,0:T(8,128)(2,1)}, u32[]{:S(2)}, u32[]{:S(2)}) collective-permute-start(bf16[256,1024]{1,0:T(8,128)(2,1)} %get-tuple-element.209), channel_id=1, source_target_pairs={{0,8},{8,0},{1,9},{9,1},{2,10},{10,2},{3,11},{11,3},{4,12},{12,4},... | collective-permute-start | bytes 1572872 | tf_op jit(solution)/shard_map/ppermute | solution.py:30
  920.0 25.7 %all-to-all-start.13 = ((bf16[4,256,768]{2,1,0:T(8,128)(2,1)}), bf16[4,256,768]{2,1,0:T(8,128)(2,1)}, u32[]{:S(2)}, u32[]{:S(2)}) async-start(bf16[4,256,768]{2,1,0:T(8,128)(2,1)} %pad_maximum_fusion.5), calls=%async_computation.13 | async-start | bytes 3145728 | tf_op jit(solution)/shard_map/all_to_all | solution.py:289
  945.7 21.6 %all-to-all-start.9 = ((bf16[4,256,640]{2,1,0:T(8,128)(2,1)}), bf16[4,256,640]{2,1,0:T(8,128)(2,1)}, u32[]{:S(2)}, u32[]{:S(2)}) async-start(bf16[4,256,640]{2,1,0:T(8,128)(2,1)} %pad_maximum_fusion.7), calls=%async_computation.9 | async-start | bytes 2621440 | tf_op jit(solution)/shard_map/all_to_all | solution.py:289
  953.5 12.5 collective-permute-start.55
  954.9 31.0 %collective-permute-start.57 = (bf16[4,128,1024]{1,2,0:T(8,128)(2,1)}, bf16[4,128,1024]{1,2,0:T(8,128)(2,1)}, u32[]{:S(2)}, u32[]{:S(2)}) collective-permute-start(bf16[4,128,1024]{1,2,0:T(8,128)(2,1)} %all-to-all-done), channel_id=1, source_target_pairs={{0,8},{8,0},{1,9},{9,1},{2,10},{10,2},{3,11},{11,3},{4,12},{12,4},... | collective-permute-start | bytes 3145736 | tf_op jit(solution)/shard_map/ppermute | solution.py:30
  967.2 11.9 all-to-all-start.1
  981.1 39.3 %all-to-all-start.12 = ((bf16[4,384,1024]{1,2,0:T(8,128)(2,1)}), bf16[4,384,1024]{1,2,0:T(8,128)(2,1)}, u32[]{:S(2)}, u32[]{:S(2)}) async-start(bf16[4,384,1024]{1,2,0:T(8,128)(2,1)} %broadcast_in_dim.52), calls=%async_computation.12 | async-start | bytes 6291456 | tf_op jit(solution)/shard_map/all_to_all | solution.py:52
  1020.4 16.0 %all-to-all-start.2 = ((bf16[16,80,256]{2,1,0:T(8,128)(2,1)}), bf16[16,80,256]{2,1,0:T(8,128)(2,1)S(1)}, u32[]{:S(2)}, u32[]{:S(2)}) async-start(bf16[16,80,256]{2,1,0:T(8,128)(2,1)} %bitcast.75), calls=%async_computation.2 | async-start | bytes 1310720 | tf_op jit(solution)/shard_map/all_to_all | solution.py:301
  1028.4 21.6 %collective-permute-start.58 = (bf16[4,128,1024]{1,2,0:T(8,128)(2,1)}, bf16[4,128,1024]{1,2,0:T(8,128)(2,1)}, u32[]{:S(2)}, u32[]{:S(2)}) collective-permute-start(bf16[4,128,1024]{1,2,0:T(8,128)(2,1)} %slice.327), channel_id=1, source_target_pairs={{0,8},{8,0},{1,9},{9,1},{2,10},{10,2},{3,11},{11,3},{4,12},{12,4},... | collective-permute-start | bytes 3145736 | tf_op jit(solution)/shard_map/ppermute | solution.py:30
  1036.4 23.8 %all-to-all-start.5 = ((bf16[4,256,768]{2,1,0:T(8,128)(2,1)}), bf16[4,256,768]{2,1,0:T(8,128)(2,1)}, u32[]{:S(2)}, u32[]{:S(2)}) async-start(bf16[4,256,768]{2,1,0:T(8,128)(2,1)} %pad_maximum_fusion.3), calls=%async_computation.5 | async-start | bytes 3145728 | tf_op jit(solution)/shard_map/all_to_all | solution.py:289
  1050.0 41.8 %collective-permute-start.59 = (bf16[4,128,1024]{1,2,0:T(8,128)(2,1)}, bf16[4,128,1024]{1,2,0:T(8,128)(2,1)}, u32[]{:S(2)}, u32[]{:S(2)}) collective-permute-start(bf16[4,128,1024]{1,2,0:T(8,128)(2,1)} %slice.335), channel_id=1, source_target_pairs={{0,8},{8,0},{1,9},{9,1},{2,10},{10,2},{3,11},{11,3},{4,12},{12,4},... | collective-permute-start | bytes 3145736 | tf_op jit(solution)/shard_map/ppermute | solution.py:30
  1059.6 32.3 %collective-permute-start.60 = (bf16[4,128,1024]{1,2,0:T(8,128)(2,1)}, bf16[4,128,1024]{1,2,0:T(8,128)(2,1)}, u32[]{:S(2)}, u32[]{:S(2)}) collective-permute-start(bf16[4,128,1024]{1,2,0:T(8,128)(2,1)} %slice.346), channel_id=1, source_target_pairs={{0,8},{8,0},{1,9},{9,1},{2,10},{10,2},{3,11},{11,3},{4,12},{12,4},... | collective-permute-start | bytes 3145736 | tf_op jit(solution)/shard_map/ppermute | solution.py:30
  1061.1 17.2 %all-to-all-start.3 = ((bf16[16,80,256]{2,1,0:T(8,128)(2,1)}), bf16[16,80,256]{2,1,0:T(8,128)(2,1)}, u32[]{:S(2)}, u32[]{:S(2)}) async-start(bf16[16,80,256]{2,1,0:T(8,128)(2,1)} %broadcast_in_dim.47), calls=%async_computation.3 | async-start | bytes 1310720 | tf_op jit(solution)/shard_map/all_to_all | solution.py:52
  1078.3 42.8 %all-to-all-start.6 = ((bf16[16,64,768]{2,1,0:T(8,128)(2,1)}), bf16[16,64,768]{2,1,0:T(8,128)(2,1)S(1)}, u32[]{:S(2)}, u32[]{:S(2)}) async-start(bf16[16,64,768]{2,1,0:T(8,128)(2,1)} %bitcast.325), calls=%async_computation.6 | async-start | bytes 3145728 | tf_op jit(solution)/shard_map/all_to_all | solution.py:301
  1121.1 25.3 %all-to-all-start.10 = ((bf16[16,64,512]{2,1,0:T(8,128)(2,1)}), bf16[16,64,512]{2,1,0:T(8,128)(2,1)}, u32[]{:S(2)}, u32[]{:S(2)}) async-start(bf16[16,64,512]{2,1,0:T(8,128)(2,1)} %bitcast.332), calls=%async_computation.10 | async-start | bytes 2097152 | tf_op jit(solution)/shard_map/all_to_all | solution.py:301
  1146.4 28.0 %all-to-all-start.14 = ((bf16[16,64,768]{2,1,0:T(8,128)(2,1)}), bf16[16,64,768]{2,1,0:T(8,128)(2,1)}, u32[]{:S(2)}, u32[]{:S(2)}) async-start(bf16[16,64,768]{2,1,0:T(8,128)(2,1)} %bitcast.326), calls=%async_computation.14 | async-start | bytes 3145728 | tf_op jit(solution)/shard_map/all_to_all | solution.py:301
  1175.8 25.8 %all-to-all-start.7 = ((bf16[16,64,768]{2,1,0:T(8,128)(2,1)}), bf16[16,64,768]{2,1,0:T(8,128)(2,1)S(1)}, u32[]{:S(2)}, u32[]{:S(2)}) async-start(bf16[16,64,768]{2,1,0:T(8,128)(2,1)} %broadcast_in_dim.49), calls=%async_computation.7 | async-start | bytes 3145728 | tf_op jit(solution)/shard_map/all_to_all | solution.py:52
  1202.7 20.8 %all-to-all-start.11 = ((bf16[16,64,512]{2,1,0:T(8,128)(2,1)}), bf16[16,64,512]{2,1,0:T(8,128)(2,1)}, u32[]{:S(2)}, u32[]{:S(2)}) async-start(bf16[16,64,512]{2,1,0:T(8,128)(2,1)} %broadcast_in_dim.51), calls=%async_computation.11 | async-start | bytes 2097152 | tf_op jit(solution)/shard_map/all_to_all | solution.py:52
  1224.9 52.2 %all-to-all-start.15 = ((bf16[16,64,768]{2,1,0:T(8,128)(2,1)}), bf16[16,64,768]{2,1,0:T(8,128)(2,1)S(1)}, u32[]{:S(2)}, u32[]{:S(2)}) async-start(bf16[16,64,768]{2,1,0:T(8,128)(2,1)} %broadcast_in_dim.53), calls=%async_computation.15 | async-start | bytes 3145728 | tf_op jit(solution)/shard_map/all_to_all | solution.py:52
  (137 other events, 1739.6 us)
